TPU v7x, 128 devices: a whole 4x4x4 slice. The times are simulated.
128 devices in a mesh: dp: 8 (over y, core), ctx: 16 (over z, x).
Axes of the slice: x: 4, y: 4, z: 4, core: 2. Of those that a mesh axis runs over, the one named last changes fastest.
Arguments:
- queries: bfloat16 [8, 16, 128, 4096], P('dp', None, 'ctx'), may hold values from -64 to 64
- key_rows: bfloat16 [8, 16, 128, 512], P('dp', None, 'ctx'), may hold values from -24 to 24
- values: bfloat16 [8, 16, 128, 512], P('dp', None, 'ctx'), may hold values from -6 to 6
- out_grad: bfloat16 [8, 16, 128, 4096], P('dp', None, 'ctx'), may hold values from -6 to 6
- out_gain: bfloat16 [4096], replicated, may hold values from 0.099609375 to 1.8984375
- documents: int32 [8, 2048], P('dp'), may hold values from 0 to 63, never falling along the last dimension, each value on 1 to 128 neighbouring positions
Outputs:
- attended: bfloat16 [8, 16, 128, 4096], P('dp', None, 'ctx')
- query_grad: bfloat16 [8, 16, 128, 4096], P('dp', None, 'ctx')
- key_grad: bfloat16 [8, 16, 128, 512], P('dp', None, 'ctx')
- value_grad: bfloat16 [8, 16, 128, 512], P('dp', None, 'ctx')
- gain_grad: float32 [4096], P('ctx')
Inputs may be any that keep to these rules, and one draw needn't show every extreme that they name: `documents`: in each sequence the document numbers never fall, and each document covers 1 to 128 consecutive positions; some document covers exactly 128.
All inputs are finite; a program needn't handle non-finite values.
Results may differ from a plain program's by a relative error of at most 0.011.
Values may be sent and summed in bfloat16 or wider, within the bound.
A program may use at most 128 MiB of HBM per device.

v0:
```python
import math

import jax
import jax.numpy as jnp
from jax import lax
from jax.sharding import PartitionSpec as P

KV_HEADS = 4
HEAD_DIM = 128
GROUP = 8


NEG_BIG = -1e30


def attend_block(q_grp, dout_grp, k_grp, v_grp, allowed):
    f32 = jnp.float32
    scale = 1.0 / math.sqrt(q_grp.shape[-1])
    scores = jnp.einsum("rqgd,rwd->rgqw", q_grp, k_grp, preferred_element_type=f32) * scale
    scores = jnp.where(allowed[:, None], scores, NEG_BIG)
    top = jnp.max(scores, axis=-1, keepdims=True)
    expo = jnp.where(allowed[:, None], jnp.exp(scores - top), 0.0)
    probs = expo / jnp.sum(expo, axis=-1, keepdims=True)
    probs_low = probs.astype(jnp.bfloat16)
    attn = jnp.einsum("rgqw,rwd->rqgd", probs_low, v_grp, preferred_element_type=f32).astype(
        jnp.bfloat16
    )
    delta = jnp.sum(dout_grp.astype(f32) * attn.astype(f32), axis=-1)
    prob_grad = jnp.einsum("rqgd,rwd->rgqw", dout_grp, v_grp, preferred_element_type=f32)
    score_grad = (probs * (prob_grad - jnp.transpose(delta, (0, 2, 1))[..., None])).astype(
        jnp.bfloat16
    )
    query_grad = (
        jnp.einsum("rgqw,rwd->rqgd", score_grad, k_grp, preferred_element_type=f32) * scale
    ).astype(jnp.bfloat16)
    key_grad = jnp.einsum("rgqw,rqgd->rwd", score_grad, q_grp, preferred_element_type=f32) * scale
    value_grad = jnp.einsum("rgqw,rqgd->rwd", probs_low, dout_grp, preferred_element_type=f32)
    return (attn, query_grad, key_grad, value_grad)


def attend_window(q_rows, dout_rows, k_win, v_win, allowed):
    rounds, width, q_width = q_rows.shape
    span, kv_width = (k_win.shape[1], k_win.shape[2])
    q_grp = jnp.moveaxis(q_rows.reshape(rounds, width, KV_HEADS, GROUP, HEAD_DIM), 2, 0)
    d_grp = jnp.moveaxis(dout_rows.reshape(rounds, width, KV_HEADS, GROUP, HEAD_DIM), 2, 0)
    k_grp = jnp.moveaxis(k_win.reshape(rounds, span, KV_HEADS, HEAD_DIM), 2, 0)
    v_grp = jnp.moveaxis(v_win.reshape(rounds, span, KV_HEADS, HEAD_DIM), 2, 0)

    def one_head(items):
        return attend_block(items[0], items[1], items[2], items[3], allowed)

    attn, query_grad, key_grad, value_grad = lax.map(one_head, (q_grp, d_grp, k_grp, v_grp))
    attn = jnp.moveaxis(attn, 0, 2).reshape(rounds, width, q_width)
    query_grad = jnp.moveaxis(query_grad, 0, 2).reshape(rounds, width, q_width)
    key_grad = jnp.moveaxis(key_grad, 0, 2).reshape(rounds, span, kv_width)
    value_grad = jnp.moveaxis(value_grad, 0, 2).reshape(rounds, span, kv_width)
    return (attn, query_grad, key_grad, value_grad)


def body(queries, key_rows, values, out_grad, out_gain, documents):
    f32 = jnp.float32
    head_grad = (out_gain.astype(f32) * out_grad.astype(f32)).astype(jnp.bfloat16)
    rounds, width = (queries.shape[1], queries.shape[2])
    ctx_count = lax.axis_size("ctx")
    place = lax.axis_index("ctx")
    tokens = width * ctx_count
    docs = documents.reshape(rounds, tokens)
    prev_docs = jnp.concatenate([jnp.full((1, tokens), -1, jnp.int32), docs[:-1]], axis=0)
    column = jnp.arange(tokens, dtype=jnp.int32)
    all_k, all_v = (
        lax.all_gather(key_rows, "ctx", axis=2, tiled=True),
        lax.all_gather(values, "ctx", axis=2, tiled=True),
    )
    zero_round = jnp.zeros_like(all_k[:, :1])
    k_win = jnp.concatenate([jnp.concatenate([zero_round, all_k[:, :-1]], axis=1), all_k], axis=2)[
        0
    ]
    v_win = jnp.concatenate([jnp.concatenate([zero_round, all_v[:, :-1]], axis=1), all_v], axis=2)[
        0
    ]
    own_cols = place * width + jnp.arange(width, dtype=jnp.int32)
    q_docs = lax.dynamic_slice_in_dim(docs, place * width, width, 1)
    doc_win = jnp.concatenate([prev_docs, docs], axis=1)
    later = jnp.concatenate(
        [jnp.ones((width, tokens), dtype=bool), column[None, :] <= own_cols[:, None]], axis=1
    )
    allowed = (doc_win[:, None, :] == q_docs[:, :, None]) & later[None]
    attn, query_grad, k_part, v_part = attend_window(
        queries[0], head_grad[0], k_win, v_win, allowed
    )
    tail = jnp.zeros_like(k_part[:1, :tokens])
    k_full = k_part[:, tokens:] + jnp.concatenate([k_part[1:, :tokens], tail], axis=0)
    v_full = v_part[:, tokens:] + jnp.concatenate([v_part[1:, :tokens], tail], axis=0)
    kv_width = k_full.shape[-1]
    k_sum, v_sum = (
        lax.psum_scatter(
            k_full.reshape(rounds, ctx_count, width, kv_width),
            "ctx",
            scatter_dimension=1,
            tiled=True,
        ),
        lax.psum_scatter(
            v_full.reshape(rounds, ctx_count, width, kv_width),
            "ctx",
            scatter_dimension=1,
            tiled=True,
        ),
    )
    key_grad = k_sum.reshape(1, rounds, width, kv_width).astype(jnp.bfloat16)
    value_grad = v_sum.reshape(1, rounds, width, kv_width).astype(jnp.bfloat16)
    attn = attn[None]
    query_grad = query_grad[None]
    attended = (out_gain.astype(f32) * attn.astype(f32)).astype(jnp.bfloat16)
    partial_sum = jnp.sum(out_grad.astype(f32) * attn.astype(f32), axis=(0, 1, 2))
    piece = lax.psum_scatter(partial_sum, "ctx", scatter_dimension=0, tiled=True)
    gain_sum = lax.psum(piece, "dp")
    gain_grad = gain_sum * (1.0 / math.sqrt(lax.axis_size("dp") * tokens * ctx_count))
    return (attended, query_grad, key_grad, value_grad, gain_grad)


def solution(mesh):
    in_specs = (
        P("dp", None, "ctx", None),
        P("dp", None, "ctx", None),
        P("dp", None, "ctx", None),
        P("dp", None, "ctx", None),
        P(),
        P("dp", None),
    )
    out_specs = (
        P("dp", None, "ctx", None),
        P("dp", None, "ctx", None),
        P("dp", None, "ctx", None),
        P("dp", None, "ctx", None),
        P("ctx"),
    )
    return jax.shard_map(body, mesh=mesh, in_specs=in_specs, out_specs=out_specs, check_vma=False)
```

profile of v0, /device:TPU:0, one launch (start us, length us, event | category | flops | bytes accessed | tf_op | source)
XLA Modules:
  0.0 425.8 jit_solution(15422326743787374731)
XLA Ops:
  16.6 41.9 %all-gather.3.cloned.1.call-done = bf16[1,16,128,512]{3,1,0,2:T(8,128)(2,1)} async-done(((bf16[1,16,8,512]{3,1,0,2:T(8,128)(2,1)}), bf16[1,16,128,512]{3,1,0,2:T(8,128)(2,1)}) %all-gather.3.cloned.1.call-update) | async-done | bytes 2097168 | tf_op jit(solution)/shard_map/all_gather | solution.py:72
  58.5 3.5 copy.44
  64.3 41.5 %all-gather.5.cloned.1.call-done = bf16[1,16,128,512]{3,1,0,2:T(8,128)(2,1)} async-done(((bf16[1,16,8,512]{3,1,0,2:T(8,128)(2,1)}), bf16[1,16,128,512]{3,1,0,2:T(8,128)(2,1)}) %all-gather.5.cloned.1.call-update) | async-done | bytes 2097168 | tf_op jit(solution)/shard_map/all_gather | solution.py:71
  105.8 3.5 copy.47
  111.6 72.2 %while.17 = (s32[]{:T(128)}, bf16[4,16,8,8,128]{4,2,3,1,0:T(8,128)(2,1)}, bf16[4,16,8,8,128]{4,2,3,1,0:T(8,128)(2,1)}, f32[4,16,256,128]{2,3,0,1:T(8,128)}, f32[...) while((s32[]{:T(128)}, ...), condition=%wide.region_4.5_spmd.clone, body=%wide.region_0.4_spmd.clone.sunk | while | flops 407043328 | bytes 25841280 | solution.py:52
  113.9 2.4 bitcast_dynamic-update-slice_fusion.4
  119.2 2.8 fusion.94
  127.2 2.4 fusion.93
  131.9 2.4 bitcast_dynamic-update-slice_fusion.4
  137.2 2.8 fusion.94
  145.3 2.4 fusion.93
  150.0 2.4 bitcast_dynamic-update-slice_fusion.4
  155.3 2.8 fusion.94
  163.3 2.4 fusion.93
  168.0 2.4 bitcast_dynamic-update-slice_fusion.4
  173.3 2.8 fusion.94
  181.4 2.4 fusion.93
  186.2 4.7 %slice_add_fusion = f32[16,128,512]{1,2,0:T(8,128)} fusion(f32[16,256,512]{1,2,0:T(8,128)} %bitcast.173, f32[15,128,512]{1,2,0:T(8,128)S(1)} %slice.37), kind=kLoop, calls=%fused_computation.57 | loop fusion | flops 1048576 | bytes 12320768 | tf_op jit(solution)/shard_map/add | solution.py:93
  190.9 5.3 %copy.58 = f32[16,128,512]{2,1,0:T(8,128)} copy(f32[16,128,512]{1,2,0:T(8,128)} %slice_add_fusion) | data formatting | bytes 8388608 | tf_op jit(solution)/shard_map/add | solution.py:93
  196.2 2.4 slice.35
  198.6 4.7 %slice_add_fusion.1 = f32[16,128,512]{1,2,0:T(8,128)} fusion(f32[16,256,512]{1,2,0:T(8,128)} %bitcast.171, f32[15,128,512]{1,2,0:T(8,128)S(1)} %slice.35), kind=kLoop, calls=%fused_computation.58 | loop fusion | flops 1048576 | bytes 12320768 | tf_op jit(solution)/shard_map/add | solution.py:92
  203.3 5.3 %copy.56 = f32[16,128,512]{2,1,0:T(8,128)} copy(f32[16,128,512]{1,2,0:T(8,128)} %slice_add_fusion.1) | data formatting | bytes 8388608 | tf_op jit(solution)/shard_map/add | solution.py:92
  211.8 189.6 %all-reduce.11 = (bf16[16,16,8,512]{3,2,1,0:T(8,128)(2,1)S(1)}, bf16[16,16,8,512]{3,2,1,0:T(8,128)(2,1)}, f32[4096]{0:T(1024)S(1)}) all-reduce(f32[16,16,8,512]{3,2,1,0:T(8,128)} %bitcast.168, f32[16,16,8,512]{3,2,1,0:T(8,128)} %bitcast.167, f32[4096]{0:T(1024)S(1)} %get-tuple-element.150), channel_id=2, replica_groups=mesh['dp'=8,'ctx'=16] {'ctx'}, use_global_device_ids=true, to_apply=%region_5.6.clone | all-reduce | flops 2101248 | bytes 12615680
  401.4 12.4 %psum.7 = f32[256]{0:T(256)S(1)} all-reduce(f32[256]{0:T(256)S(1)} %dynamic-slice.5), channel_id=1, replica_groups=mesh['dp'=8,'ctx'=16] {'dp'}, use_global_device_ids=true, to_apply=%region_9.10 | all-reduce | flops 256 | bytes 2048 | tf_op jit(solution)/shard_map/psum | solution.py:116
  (77 shorter events, 65.4 us)
Async XLA Ops:
  7.2 8.0 %copy-start.3 = (u32[128]{0:T(128)S(1)}, u32[128]{0:T(128)}, u32[]{:S(2)}) copy-start(u32[128]{0:T(128)} %constant.69) | copy-start | bytes 1540
  7.2 6.7 %copy-start.1 = (bf16[1,16,8,4096]{3,2,1,0:T(8,128)(2,1)S(1)}, bf16[1,16,8,4096]{3,2,1,0:T(8,128)(2,1)}, u32[]{:S(2)}) copy-start(bf16[1,16,8,4096]{3,2,1,0:T(8,128)(2,1)} %param.8) | copy-start | bytes 3145732
  7.2 9.3 %copy-start.2 = (s32[1,2048]{1,0:T(1,128)S(1)}, s32[1,2048]{1,0:T(1,128)}, u32[]{:S(2)}) copy-start(s32[1,2048]{1,0:T(1,128)} %param.13) | copy-start | bytes 24580
  7.2 51.3 %all-gather.3.cloned.1.call-start = ((), (), s32[]{:S(2)}) async-start(), calls=%async_computation | async-start | bytes 2228224 | tf_op jit(solution)/shard_map/all_gather | solution.py:72
  8.9 96.8 %all-gather.5.cloned.1.call-start = ((), (), s32[]{:S(2)}) async-start(), calls=%async_computation.1 | async-start | bytes 2228224 | tf_op jit(solution)/shard_map/all_gather | solution.py:71
  208.7 1.8 copy-start
Sparse Core Ops, SparseCore 0:
  10.7 47.7 all-gather.2
  61.2 44.5 all-gather.4
where the time goes:
time: 428 us; the launch traced here: 426 us
  blocking collectives  202 us (47%)
  waiting for transfers between devices  83.4 us (19%)
  matrix products  52.1 us (12%)
  local copies, waits for them, and re-layouts  47.9 us (11%)
  other arithmetic  25.3 us (6%)
  between operations  14.9 us (3%)
    unnamed x1, blocking collectives  190 us
    all_gather x1, waiting for transfers between devices, body(): lax.all_gather(values, 'ctx', axis=2, tiled=True)  41.9 us
    all_gather x1, waiting for transfers between devices, body(): lax.all_gather(key_rows, 'ctx', axis=2, tiled=True)  41.5 us
    dynamic_update_slice x8, local copies, waits for them, and re-layouts, attend_window(): lax.map(one_head, (q_grp, d_grp, k_grp, v_grp))  13.8 us
    psum x1, blocking collectives, body(): gain_sum = lax.psum(piece, 'dp')  12.4 us
    dot_general x4, matrix products, attend_block(): jnp.einsum('rgqw,rqgd->rwd', score_grad, q_grp, preferred_element_type=f32)  11.3 us
    dot_general x4, matrix products, attend_block(): jnp.einsum('rgqw,rwd->rqgd', probs_low, v_grp, preferred_element_type=f32)  9.68 us
    dot_general x4, matrix products, attend_block(): jnp.einsum('rgqw,rwd->rqgd', score_grad, k_grp, preferred_element_type=f32)  9.63 us
  transfers between devices with their start and end apart: 2, of which 2 were waited for; matrix products, arithmetic and copies ran while one was open for 3% of the time, Pallas kernels for 0%

commit v1 on v0

v1 whole, which is shorter than its diff:
```python
import functools
import math

import jax
import jax.numpy as jnp
from jax import lax
from jax.experimental import pallas as pl
from jax.experimental.pallas import tpu as pltpu
from jax.sharding import PartitionSpec as P

MESH = pl.DeviceIdType.MESH
F32 = jnp.float32
BF16 = jnp.bfloat16
SIDE = 4
ROUNDS = 16
OWN = ROUNDS // SIDE
SLOTS = OWN + 1
WIDE = 8
DIM = 128
GROUP = 8
HEADS = 4
TOK = 128
ROWS = SIDE * WIDE * GROUP
NEG_BIG = -1e30
UNIT_HEAD = (0, 2, 1, 3)


def dot_t(a, b):
    return lax.dot_general(a, b, (((1,), (1,)), ((), ())), preferred_element_type=F32)


def dot_tn(a, b):
    return lax.dot_general(a, b, (((0,), (0,)), ((), ())), preferred_element_type=F32)


def dot_n(a, b):
    return lax.dot_general(a, b, (((1,), (0,)), ((), ())), preferred_element_type=F32)


def kernel(
    q_hbm, k_hbm, v_hbm, g_hbm, gain_ref, docs_ref,
    att_hbm, dq_hbm, dk_ref, dv_ref, gg_ref,
    qin, gin, kin, vin, att_o, dq_o, kp, vp, kr, vr, ks, vs, ka, va,
    le_ref, bias_ref, kacc, vacc, gacc, gsend, grecv, gsum, gdp,
    kv_send, kv_recv, kvg_send, kvg_recv, q_send, q_recv, out_send, out_recv,
    rs_send, rs_recv, aa_send, aa_recv, g_send, g_recv, d_send, d_recv,
):
    dp = lax.axis_index("dp")
    ctx = lax.axis_index("ctx")
    z = ctx // SIDE
    x = ctx % SIDE
    scale = 1.0 / math.sqrt(DIM)

    def at_ctx(c):
        return (dp, c)

    def a_peer(t, k):
        a = ((x if t == 0 else z) + k) % SIDE
        return a, at_ctx(z * SIDE + a if t == 0 else a * SIDE + x)

    def g_peer(t, k):
        g = ((z if t == 0 else x) + k) % SIDE
        return g, at_ctx(g * SIDE + x if t == 0 else z * SIDE + g)

    def me_a(t):
        return x if t == 0 else z

    def me_g(t):
        return z if t == 0 else x

    def off(a):
        return (a + SIDE - 1) // SIDE

    def remote(src, dst, ssem, rsem, dev):
        pltpu.make_async_remote_copy(
            src_ref=src, dst_ref=dst, send_sem=ssem, recv_sem=rsem, device_id=dev, device_id_type=MESH
        ).start()

    def local(src, dst, sem):
        pltpu.make_async_copy(src, dst, sem).start()

    def drain(ref, sem):
        pltpu.make_async_copy(ref, ref, sem).wait()

    barrier = pltpu.get_barrier_semaphore()
    for i in range(1, 16):
        pl.semaphore_signal(barrier, inc=1, device_id=at_ctx((ctx + i) % 16), device_id_type=MESH)
    for i in range(1, 8):
        pl.semaphore_signal(barrier, inc=1, device_id=((dp + i) % 8, ctx), device_id_type=MESH)

    def kv_local(u):
        t, h = u % 2, UNIT_HEAD[u]
        a = me_a(t)
        lanes = pl.ds(h * DIM, DIM)
        for n, (src, dst) in enumerate(((k_hbm, kin), (v_hbm, vin))):
            local(src.at[0, pl.ds(OWN * a - off(a), SLOTS), :, lanes], dst.at[u, me_g(t), a], kv_recv.at[u, n])

    def q_local(u):
        t, h = u % 2, UNIT_HEAD[u]
        a = me_a(t)
        lanes = pl.ds(h * GROUP * DIM, GROUP * DIM)
        for n, (src, dst) in enumerate(((q_hbm, qin), (g_hbm, gin))):
            local(src.at[0, pl.ds(OWN * a, OWN), :, lanes], dst.at[u, a], q_recv.at[u, n])

    def kv_first(u):
        t, h = u % 2, UNIT_HEAD[u]
        lanes = pl.ds(h * DIM, DIM)
        for k in (1, 3, 2):
            a, dev = a_peer(t, k)
            for n, (src, dst) in enumerate(((k_hbm, kin), (v_hbm, vin))):
                remote(
                    src.at[0, pl.ds(OWN * a - off(a), SLOTS), :, lanes], dst.at[u, me_g(t), me_a(t)],
                    kv_send.at[n], kv_recv.at[u, n], dev,
                )

    def kv_gather(u):
        t = u % 2
        for n, buf in enumerate((kin, vin)):
            drain(buf.at[u, 0], kv_recv.at[u, n])
        for k in (1, 3, 2):
            _, dev = g_peer(t, k)
            for n, buf in enumerate((kin, vin)):
                remote(buf.at[u, me_g(t)], buf.at[u, me_g(t)], kvg_send.at[n], kvg_recv.at[u, n], dev)

    def q_send_all(u):
        t, h = u % 2, UNIT_HEAD[u]
        lanes = pl.ds(h * GROUP * DIM, GROUP * DIM)
        for k in (1, 3, 2):
            a, dev = a_peer(t, k)
            for n, (src, dst) in enumerate(((q_hbm, qin), (g_hbm, gin))):
                remote(
                    src.at[0, pl.ds(OWN * a, OWN), :, lanes], dst.at[u, me_a(t)], q_send.at[n], q_recv.at[u, n], dev
                )

    for u in range(4):
        kv_local(u)
    for u in range(4):
        q_local(u)
    pl.semaphore_wait(barrier, 22)
    for u in range(4):
        kv_first(u)
    for u in (0, 1):
        q_send_all(u)
    for u in range(4):
        kv_gather(u)
    for u in (2, 3):
        q_send_all(u)

    key_i = lax.broadcasted_iota(jnp.int32, (TOK, ROWS), 0)
    row_i = lax.broadcasted_iota(jnp.int32, (TOK, ROWS), 1) & (SIDE * WIDE - 1)
    for t in range(2):
        def key_col(i):
            return i if t == 0 else ((i >> 3) & 3) * 32 + (i >> 5) * 8 + (i & 7)

        def row_col(i):
            i = i & (SIDE * WIDE - 1)
            return z * 32 + i if t == 0 else (i >> 3) * 32 + x * 8 + (i & 7)

        le = key_col(key_i) <= row_col(row_i)
        le_ref[t] = jnp.where(le, 1.0, 0.0)
        perm = jnp.where(
            key_col(lax.broadcasted_iota(jnp.int32, (TOK, TOK), 0)) == lax.broadcasted_iota(jnp.int32, (TOK, TOK), 1),
            1.0, 0.0,
        ).astype(BF16)
        sel = jnp.where(
            row_col(lax.broadcasted_iota(jnp.int32, (ROWS, TOK), 0)) == lax.broadcasted_iota(jnp.int32, (ROWS, TOK), 1),
            1.0, 0.0,
        ).astype(BF16)

        def doc_row(r):
            return docs_ref[0:1, pl.ds(pl.multiple_of(r * TOK, TOK), TOK)].astype(F32)

        def one_bias(r, _):
            rho = me_a(t) * OWN + r
            cur = doc_row(rho)
            prev = doc_row((rho + ROUNDS - 1) % ROUNDS)
            k_cur = dot_t(perm, jnp.broadcast_to(cur, (ROWS, TOK)).astype(BF16))
            k_prev = dot_t(perm, jnp.broadcast_to(prev, (ROWS, TOK)).astype(BF16))
            q_doc = dot_t(jnp.broadcast_to(cur, (TOK, TOK)).astype(BF16), sel)
            k_prev = jnp.where(rho > 0, k_prev, -1.0)
            mine = jnp.where(le_ref[t] > 0.5, k_cur, k_prev)
            bias_ref[t, r] = jnp.where(mine == q_doc, 0.0, NEG_BIG)
            return 0

        lax.fori_loop(0, OWN, one_bias, 0)

    def unit(u):
        t, h = u % 2, UNIT_HEAD[u]
        a = me_a(t)
        lanes = pl.ds(h * GROUP * DIM, GROUP * DIM)
        for n, buf in enumerate((qin, gin)):
            drain(buf.at[u], q_recv.at[u, n])
        for n, buf in enumerate((kin, vin)):
            drain(buf.at[u, pl.ds(0, SIDE - 1)], kvg_recv.at[u, n])
        kacc[...] = jnp.zeros_like(kacc)
        vacc[...] = jnp.zeros_like(vacc)
        gacc[...] = jnp.zeros_like(gacc)

        def one_round(r, _):
            here = r + off(a)
            before = (here + SLOTS - 1) % SLOTS

            def keys(buf, s):
                return buf[u, :, :, s].astype(F32).reshape(TOK, DIM)

            k_win = jnp.concatenate([keys(kin, here), keys(kin, before)], axis=0).astype(BF16)
            v_win = jnp.concatenate([keys(vin, here), keys(vin, before)], axis=0).astype(BF16)
            q_rows = jnp.concatenate(
                [qin[u, :, r, :, g * DIM : (g + 1) * DIM].astype(F32).reshape(SIDE * WIDE, DIM) for g in range(GROUP)],
                axis=0,
            ).astype(BF16)
            hg = jnp.concatenate(
                [
                    gin[u, :, r, :, g * DIM : (g + 1) * DIM].astype(F32).reshape(SIDE * WIDE, DIM)
                    * gain_ref[h * GROUP + g : h * GROUP + g + 1, :]
                    for g in range(GROUP)
                ],
                axis=0,
            ).astype(BF16)
            le = le_ref[t] > 0.5
            s_all = dot_t(k_win, q_rows)
            s = jnp.where(le, s_all[:TOK], s_all[TOK:]) * (scale * math.log2(math.e)) + bias_ref[t, r]
            e = jnp.exp2(s - jnp.max(s, axis=0, keepdims=True))
            p = e * (1.0 / jnp.sum(e, axis=0, keepdims=True))
            d_all = dot_t(v_win, hg)
            d = jnp.where(le, d_all[:TOK], d_all[TOK:])
            ds = p * (d - jnp.sum(p * d, axis=0, keepdims=True))
            p2 = jnp.concatenate([jnp.where(le, p, 0.0), jnp.where(le, 0.0, p)], axis=0).astype(BF16)
            ds2 = jnp.concatenate([jnp.where(le, ds, 0.0), jnp.where(le, 0.0, ds)], axis=0).astype(BF16)
            attn = dot_tn(p2, v_win).astype(BF16).astype(F32)
            dq = dot_tn(ds2, k_win) * scale
            dv = dot_n(p2, hg)
            dk = dot_n(ds2, q_rows) * scale
            for g in range(GROUP):
                rows = slice(g * SIDE * WIDE, (g + 1) * SIDE * WIDE)
                cols = slice(g * DIM, (g + 1) * DIM)
                a_g = attn[rows].reshape(SIDE, WIDE, DIM)
                gacc[g] += jnp.sum(a_g * gin[u, :, r, :, cols].astype(F32), axis=0)
                att_o[u, :, r, :, cols] = (a_g * gain_ref[h * GROUP + g : h * GROUP + g + 1, :]).astype(BF16)
                dq_o[u, :, r, :, cols] = dq[rows].reshape(SIDE, WIDE, DIM).astype(BF16)
            kp[u, :, :, before] = (kacc[...] + dk[TOK:]).reshape(SIDE, SIDE, WIDE, DIM).astype(BF16)
            vp[u, :, :, before] = (vacc[...] + dv[TOK:]).reshape(SIDE, SIDE, WIDE, DIM).astype(BF16)
            kacc[...] = dk[:TOK]
            vacc[...] = dv[:TOK]
            for n, (buf, dst) in enumerate(((att_o, att_hbm), (dq_o, dq_hbm))):
                for k in (1, 3, 2):
                    b, dev = a_peer(t, k)
                    remote(
                        buf.at[u, b, r], dst.at[0, OWN * a + r, :, lanes], out_send.at[n], out_recv.at[n], dev
                    )
                local(buf.at[u, a, r], dst.at[0, OWN * a + r, :, lanes], out_recv.at[n])
            return 0

        lax.fori_loop(0, OWN, one_round, 0)
        last = OWN - 1 + off(a)
        kp[u, :, :, last] = kacc[...].reshape(SIDE, SIDE, WIDE, DIM).astype(BF16)
        vp[u, :, :, last] = vacc[...].reshape(SIDE, SIDE, WIDE, DIM).astype(BF16)
        for k in (1, 3, 2):
            g, dev = g_peer(t, k)
            for n, (src, dst) in enumerate(((kp, kr), (vp, vr))):
                remote(src.at[u, g], dst.at[u, k - 1], rs_send.at[n], rs_recv.at[u, n], dev)
        for i in range(SIDE):
            for j in range(2):
                gsend[u, i, j : j + 1, :] = jnp.sum(gacc[2 * i + j], axis=0, keepdims=True)
        for i in range(SIDE):
            owner = h * SIDE + i

            @pl.when(owner != ctx)
            def _():
                remote(gsend.at[u, i], grecv.at[(ctx - owner + 15) % 16], g_send, g_recv, at_ctx(owner))

    def reduce_back(u):
        t = u % 2
        for n, (part, got, total, back) in enumerate(((kp, kr, ks, ka), (vp, vr, vs, va))):
            drain(got.at[u], rs_recv.at[u, n])
            acc = part[u, me_g(t)].astype(F32)
            for k in range(SIDE - 1):
                acc += got[u, k].astype(F32)
            total[u] = acc.astype(BF16)
            for k in (1, 3, 2):
                b, dev = a_peer(t, k)
                remote(total.at[u, b], back.at[u, me_a(t)], aa_send.at[n], aa_recv.at[u, n], dev)
            local(total.at[u, me_a(t)], back.at[u, me_a(t)], aa_recv.at[u, n])

    def finish(u):
        h = UNIT_HEAD[u]
        cols = slice(h * DIM, (h + 1) * DIM)
        for n, (back, out) in enumerate(((ka, dk_ref), (va, dv_ref))):
            drain(back.at[u], aa_recv.at[u, n])
            for rho in range(ROUNDS):
                b, r = rho // OWN, rho % OWN
                val = back[u, b, r if b == 0 else r + 1]
                if r == OWN - 1 and b < SIDE - 1:
                    val = (val.astype(F32) + back[u, b + 1, 0].astype(F32)).astype(BF16)
                out[0, rho, :, cols] = val

    gsend[...] = jnp.zeros_like(gsend)
    for u in range(4):
        unit(u)
        if u >= 1:
            reduce_back(u - 1)
    drain(grecv.at[pl.ds(0, 15)], g_recv)
    total = jnp.zeros((8, DIM), F32)
    for u in range(4):
        for i in range(SIDE):
            total += jnp.where(UNIT_HEAD[u] * SIDE + i == ctx, gsend[u, i], 0.0)
    for i in range(15):
        total += grecv[i]
    gsum[...] = total
    for i in range(1, 8):
        remote(gsum, gdp.at[i - 1], d_send, d_recv, ((dp + i) % 8, ctx))
    reduce_back(3)
    for u in range(3):
        finish(u)
    drain(gdp.at[pl.ds(0, 7)], d_recv)
    total = gsum[...]
    for i in range(7):
        total += gdp[i]
    gg_ref[...] = total[:2] * (1.0 / 128.0)
    finish(3)
    for n, buf in enumerate((kin, vin)):
        drain(buf.at[:, 0, pl.ds(0, SIDE - 1)], kv_send.at[n])
        drain(buf.at[:, pl.ds(0, SIDE - 1)], kvg_send.at[n])
    for n, buf in enumerate((qin, gin)):
        drain(buf.at[:, pl.ds(0, SIDE - 1)], q_send.at[n])
    for n, buf in enumerate((kr, vr)):
        drain(buf, rs_send.at[n])
    for n, buf in enumerate((ka, va)):
        drain(buf.at[:, pl.ds(0, SIDE - 1)], aa_send.at[n])
    for n, (buf, dst) in enumerate(((att_o, att_hbm), (dq_o, dq_hbm))):
        drain(buf.at[:, pl.ds(0, SIDE - 1)], out_send.at[n])
        drain(dst, out_recv.at[n])
    drain(grecv.at[pl.ds(0, 15)], g_send)
    drain(gdp.at[pl.ds(0, 7)], d_send)


def body(queries, key_rows, values, out_grad, out_gain, documents):
    gain = out_gain.reshape(HEADS * GROUP, DIM).astype(F32)
    any_spec = pl.BlockSpec(memory_space=pl.ANY)
    vmem = pl.BlockSpec(memory_space=pltpu.VMEM)
    wide = pltpu.VMEM((4, SIDE, OWN, WIDE, GROUP * DIM), BF16)
    narrow = pltpu.VMEM((4, SIDE, SIDE, SLOTS, WIDE, DIM), BF16)
    narrow3 = pltpu.VMEM((4, SIDE - 1, SIDE, SLOTS, WIDE, DIM), BF16)
    flat = pltpu.VMEM((4, SIDE, SLOTS, WIDE, DIM), BF16)
    dma = pltpu.SemaphoreType.DMA
    att, dq, dk, dv, gg = pl.pallas_call(
        kernel,
        out_shape=(
            jax.ShapeDtypeStruct(queries.shape, BF16),
            jax.ShapeDtypeStruct(queries.shape, BF16),
            jax.ShapeDtypeStruct(key_rows.shape, BF16),
            jax.ShapeDtypeStruct(key_rows.shape, BF16),
            jax.ShapeDtypeStruct((2, DIM), F32),
        ),
        in_specs=[any_spec, any_spec, any_spec, any_spec, vmem, vmem],
        out_specs=(any_spec, any_spec, vmem, vmem, vmem),
        scratch_shapes=[
            wide, wide, narrow, narrow, wide, wide, narrow, narrow, narrow3, narrow3, flat, flat, flat, flat,
            pltpu.VMEM((2, TOK, ROWS), F32),
            pltpu.VMEM((2, OWN, TOK, ROWS), F32),
            pltpu.VMEM((TOK, DIM), F32),
            pltpu.VMEM((TOK, DIM), F32),
            pltpu.VMEM((GROUP, WIDE, DIM), F32),
            pltpu.VMEM((4, SIDE, 8, DIM), F32),
            pltpu.VMEM((15, 8, DIM), F32),
            pltpu.VMEM((8, DIM), F32),
            pltpu.VMEM((7, 8, DIM), F32),
            dma((2,)), dma((4, 2)), dma((2,)), dma((4, 2)), dma((2,)), dma((4, 2)), dma((2,)), dma((2,)),
            dma((2,)), dma((4, 2)), dma((2,)), dma((4, 2)), dma, dma, dma, dma,
        ],
        compiler_params=pltpu.CompilerParams(
            collective_id=0, has_side_effects=True, vmem_limit_bytes=48 * 1024 * 1024
        ),
        name="packed_attention",
    )(queries, key_rows, values, out_grad, gain, documents)
    return att, dq, dk, dv, gg.reshape(2 * DIM)


def solution(mesh):
    tokens = P("dp", None, "ctx", None)
    return jax.shard_map(
        body,
        mesh=mesh,
        in_specs=(tokens, tokens, tokens, tokens, P(), P("dp", None)),
        out_specs=(tokens, tokens, tokens, tokens, P("ctx")),
        check_vma=False,
    )
```

time: 428 us -> 63.8 us (0.15)
  blocking collectives: 202 us -> 0 us
  waiting for transfers between devices: 83.4 us -> 0 us
  Pallas kernels: 0 us -> 54.1 us
  matrix products: 52.1 us -> 0 us
  local copies, waits for them, and re-layouts: 47.9 us -> 8.07 us
  other arithmetic: 25.3 us -> 0.71 us
  between operations: 14.9 us -> 0.65 us
    unnamed x1 -> x0, blocking collectives: 190 us -> none
    all_gather x2 -> x0, waiting for transfers between devices: 83.4 us -> none  [the longest x1 41.9 us: body(): lax.all_gather(values, 'ctx', axis=2, tiled=True)]
    pallas_call x0 -> x1, Pallas kernels: none -> 54.1 us  [body(): pl.pallas_call(kernel, out_shape=(jax.ShapeDtypeStruct(queries.shape, BF1...]
    dot_general x20 -> x0, matrix products: 44.3 us -> none  [the longest x4 11.3 us: attend_block(): jnp.einsum('rgqw,rqgd->rwd', score_grad, q_grp, preferred_element_type=f32)]
    dynamic_update_slice x8 -> x0, local copies, waits for them, and re-layouts: 13.8 us -> none  [attend_window(): lax.map(one_head, (q_grp, d_grp, k_grp, v_grp))]
    psum x1 -> x0, blocking collectives: 12.4 us -> none  [body(): gain_sum = lax.psum(piece, 'dp')]
    add x2 -> x0, local copies, waits for them, and re-layouts: 10.7 us -> none  [the longest x1 5.35 us: body(): k_part[:, tokens:] + jnp.concatenate([k_part[1:, :tokens], tail], axis=0)]
    add x3 -> x0, other arithmetic: 9.41 us -> none  [the longest x1 4.72 us: body(): k_part[:, tokens:] + jnp.concatenate([k_part[1:, :tokens], tail], axis=0)]
  transfers between devices with their start and end apart: 2 -> 0, of which waited for: 2 -> 0; matrix products, arithmetic and copies ran while one was open for 3% -> 0% of each run, Pallas kernels for 0% -> 0%
where the time goes in v1:
time: 63.8 us; the launch traced here: 63.5 us
  Pallas kernels  54.1 us (85%)
  local copies, waits for them, and re-layouts  8.07 us (13%)
  other arithmetic  0.71 us (1%)
  between operations  0.65 us (1%)
    pallas_call x1, Pallas kernels, body(): pl.pallas_call(kernel, out_shape=(jax.ShapeDtypeStruct(queries.shape, BF1...  54.1 us
    unnamed x15, local copies, waits for them, and re-layouts  8.07 us

profile of v1, /device:TPU:0, one launch (start us, length us, event | category | flops | bytes accessed | tf_op | source)
XLA Modules:
  0.0 63.5 jit_solution(6321738985600897748)
XLA Ops:
  0.6 0.0 copy-start.4
  0.6 0.7 %bitcast_convert_fusion.gain_ref = f32[32,128]{1,0:T(8,128)S(1)} fusion(bf16[4096]{0:T(1024)(128)(2,1)} %param.10), kind=kLoop, calls=%fused_computation | loop fusion | flops 4096 | bytes 24576 | tf_op jit(solution)/shard_map/convert_element_type | solution.py:338
  1.3 0.0 copy-done.4
  1.4 0.0 copy-start
  1.4 1.2 %copy-done = bf16[1,16,8,4096]{3,2,1,0:T(8,128)(2,1)S(1)} copy-done((bf16[1,16,8,4096]{3,2,1,0:T(8,128)(2,1)S(1)}, bf16[1,16,8,4096]{3,2,1,0:T(8,128)(2,1)}, u32[]{:S(2)}) %copy-start) | copy-done | bytes 1048600
  2.6 0.0 copy-start.1
  2.6 1.2 %copy-done.1 = bf16[1,16,8,4096]{3,2,1,0:T(8,128)(2,1)S(1)} copy-done((bf16[1,16,8,4096]{3,2,1,0:T(8,128)(2,1)S(1)}, bf16[1,16,8,4096]{3,2,1,0:T(8,128)(2,1)}, u32[]{:S(2)}) %copy-start.1) | copy-done | bytes 1048600
  3.8 0.0 copy-start.2
  3.8 0.9 %copy-done.2 = bf16[1,16,8,512]{3,2,1,0:T(8,128)(2,1)S(1)} copy-done((bf16[1,16,8,512]{3,2,1,0:T(8,128)(2,1)S(1)}, bf16[1,16,8,512]{3,2,1,0:T(8,128)(2,1)}, u32[]{:S(2)}) %copy-start.2) | copy-done | bytes 131096
  4.7 0.0 copy-start.3
  4.7 0.9 %copy-done.3 = bf16[1,16,8,512]{3,2,1,0:T(8,128)(2,1)S(1)} copy-done((bf16[1,16,8,512]{3,2,1,0:T(8,128)(2,1)S(1)}, bf16[1,16,8,512]{3,2,1,0:T(8,128)(2,1)}, u32[]{:S(2)}) %copy-start.3) | copy-done | bytes 131096
  5.6 54.1 %packed_attention.1 = (bf16[1,16,8,4096]{3,2,1,0:T(8,128)(2,1)S(1)}, bf16[1,16,8,4096]{3,2,1,0:T(8,128)(2,1)S(1)}, bf16[1,16,8,512]{3,2,1,0:T(8,128)(2,1)S(1)}, ...) custom-call(bf16[1,16,8,4096]{3,2,1,0:T(8,128)(2,1)S(1)} %copy-done, bf16[1,16,8,512]{3,2,1,0:T(8,128)(2,1)S(1)} %copy-done.2, ...), custom_call_target="tpu_custom_call" | custom-call | tf_op jit(solution)/shard_map/packed_attention/pallas_call | solution.py:346
  59.7 1.0 %copy.16 = bf16[1,16,8,4096]{3,2,1,0:T(8,128)(2,1)} copy(bf16[1,16,8,4096]{3,2,1,0:T(8,128)(2,1)S(1)} %get-tuple-element.20) | data formatting | bytes 2097152
  60.7 1.0 %copy.17 = bf16[1,16,8,4096]{3,2,1,0:T(8,128)(2,1)} copy(bf16[1,16,8,4096]{3,2,1,0:T(8,128)(2,1)S(1)} %get-tuple-element.21) | data formatting | bytes 2097152
  61.7 0.7 %copy.18 = bf16[1,16,8,512]{3,2,1,0:T(8,128)(2,1)} copy(bf16[1,16,8,512]{3,2,1,0:T(8,128)(2,1)S(1)} %get-tuple-element.22) | data formatting | bytes 262144
  62.3 0.7 %copy.19 = bf16[1,16,8,512]{3,2,1,0:T(8,128)(2,1)} copy(bf16[1,16,8,512]{3,2,1,0:T(8,128)(2,1)S(1)} %get-tuple-element.23) | data formatting | bytes 262144
  63.0 0.6 copy.20
Async XLA Ops:
  0.6 0.7 %copy-start.4 = (s32[1,2048]{1,0:T(1,128)S(1)}, s32[1,2048]{1,0:T(1,128)}, u32[]{:S(2)}) copy-start(s32[1,2048]{1,0:T(1,128)} %docs_ref.1) | copy-start | bytes 24580
  1.4 1.2 %copy-start = (bf16[1,16,8,4096]{3,2,1,0:T(8,128)(2,1)S(1)}, bf16[1,16,8,4096]{3,2,1,0:T(8,128)(2,1)}, u32[]{:S(2)}) copy-start(bf16[1,16,8,4096]{3,2,1,0:T(8,128)(2,1)} %q_hbm.1) | copy-start | bytes 3145732
  2.6 1.2 %copy-start.1 = (bf16[1,16,8,4096]{3,2,1,0:T(8,128)(2,1)S(1)}, bf16[1,16,8,4096]{3,2,1,0:T(8,128)(2,1)}, u32[]{:S(2)}) copy-start(bf16[1,16,8,4096]{3,2,1,0:T(8,128)(2,1)} %g_hbm.1) | copy-start | bytes 3145732
  3.8 0.9 %copy-start.2 = (bf16[1,16,8,512]{3,2,1,0:T(8,128)(2,1)S(1)}, bf16[1,16,8,512]{3,2,1,0:T(8,128)(2,1)}, u32[]{:S(2)}) copy-start(bf16[1,16,8,512]{3,2,1,0:T(8,128)(2,1)} %k_hbm.1) | copy-start | bytes 393220
  4.7 0.9 %copy-start.3 = (bf16[1,16,8,512]{3,2,1,0:T(8,128)(2,1)S(1)}, bf16[1,16,8,512]{3,2,1,0:T(8,128)(2,1)}, u32[]{:S(2)}) copy-start(bf16[1,16,8,512]{3,2,1,0:T(8,128)(2,1)} %v_hbm.1) | copy-start | bytes 393220

commit v2 on v1

--- a/solution.py
+++ b/solution.py
@@ -38,12 +38,12 @@
 
 
 def kernel(
-    q_hbm, k_hbm, v_hbm, g_hbm, gain_ref, docs_ref,
+    q_hbm, k_hbm, v_hbm, g_hbm, gain_hbm, docs_hbm,
     att_hbm, dq_hbm, dk_ref, dv_ref, gg_ref,
     qin, gin, kin, vin, att_o, dq_o, kp, vp, kr, vr, ks, vs, ka, va,
-    le_ref, bias_ref, kacc, vacc, gacc, gsend, grecv, gsum, gdp,
+    gain_ref, docs_ref, le_ref, bias_ref, kacc, vacc, gacc, gains, gpart, ghalf, gsum, gside, gfin, gdp,
     kv_send, kv_recv, kvg_send, kvg_recv, q_send, q_recv, out_send, out_recv,
-    rs_send, rs_recv, aa_send, aa_recv, g_send, g_recv, d_send, d_recv,
+    rs_send, rs_recv, aa_send, aa_recv, gr_send, gr_recv, ga_send, ga_recv, d_send, d_recv, small,
 ):
     dp = lax.axis_index("dp")
     ctx = lax.axis_index("ctx")
@@ -83,8 +83,9 @@
         pltpu.make_async_copy(ref, ref, sem).wait()
 
     barrier = pltpu.get_barrier_semaphore()
-    for i in range(1, 16):
-        pl.semaphore_signal(barrier, inc=1, device_id=at_ctx((ctx + i) % 16), device_id_type=MESH)
+    for t in range(2):
+        for k in range(1, SIDE):
+            pl.semaphore_signal(barrier, inc=1, device_id=a_peer(t, k)[1], device_id_type=MESH)
     for i in range(1, 8):
         pl.semaphore_signal(barrier, inc=1, device_id=((dp + i) % 8, ctx), device_id_type=MESH)
 
@@ -132,11 +133,13 @@
                     src.at[0, pl.ds(OWN * a, OWN), :, lanes], dst.at[u, me_a(t)], q_send.at[n], q_recv.at[u, n], dev
                 )
 
+    local(gain_hbm, gain_ref, small.at[0])
+    local(docs_hbm, docs_ref, small.at[1])
     for u in range(4):
         kv_local(u)
     for u in range(4):
         q_local(u)
-    pl.semaphore_wait(barrier, 22)
+    pl.semaphore_wait(barrier, 13)
     for u in range(4):
         kv_first(u)
     for u in (0, 1):
@@ -146,6 +149,10 @@
     for u in (2, 3):
         q_send_all(u)
 
+    drain(gain_ref, small.at[0])
+    drain(docs_ref, small.at[1])
+    for i in range(HEADS * GROUP):
+        gains[i : i + 1, :] = gain_ref[pl.ds(i * DIM, DIM)].astype(F32).reshape(1, DIM)
     key_i = lax.broadcasted_iota(jnp.int32, (TOK, ROWS), 0)
     row_i = lax.broadcasted_iota(jnp.int32, (TOK, ROWS), 1) & (SIDE * WIDE - 1)
     for t in range(2):
@@ -184,10 +191,21 @@
 
         lax.fori_loop(0, OWN, one_bias, 0)
 
-    def unit(u):
+    def bulk(u, r, count):
         t, h = u % 2, UNIT_HEAD[u]
         a = me_a(t)
         lanes = pl.ds(h * GROUP * DIM, GROUP * DIM)
+        rounds = pl.ds(r, count)
+        for n, (buf, dst) in enumerate(((att_o, att_hbm), (dq_o, dq_hbm))):
+            there = dst.at[0, pl.ds(OWN * a + r, count), :, lanes]
+            for k in (1, 3, 2):
+                b, dev = a_peer(t, k)
+                remote(buf.at[u, b, rounds], there, out_send.at[n], out_recv.at[n], dev)
+            local(buf.at[u, a, rounds], there, out_recv.at[n])
+
+    def unit(u):
+        t, h = u % 2, UNIT_HEAD[u]
+        a = me_a(t)
         for n, buf in enumerate((qin, gin)):
             drain(buf.at[u], q_recv.at[u, n])
         for n, buf in enumerate((kin, vin)):
@@ -212,7 +230,7 @@
             hg = jnp.concatenate(
                 [
                     gin[u, :, r, :, g * DIM : (g + 1) * DIM].astype(F32).reshape(SIDE * WIDE, DIM)
-                    * gain_ref[h * GROUP + g : h * GROUP + g + 1, :]
+                    * gains[h * GROUP + g : h * GROUP + g + 1, :]
                     for g in range(GROUP)
                 ],
                 axis=0,
@@ -236,19 +254,14 @@
                 cols = slice(g * DIM, (g + 1) * DIM)
                 a_g = attn[rows].reshape(SIDE, WIDE, DIM)
                 gacc[g] += jnp.sum(a_g * gin[u, :, r, :, cols].astype(F32), axis=0)
-                att_o[u, :, r, :, cols] = (a_g * gain_ref[h * GROUP + g : h * GROUP + g + 1, :]).astype(BF16)
+                att_o[u, :, r, :, cols] = (a_g * gains[h * GROUP + g : h * GROUP + g + 1, :]).astype(BF16)
                 dq_o[u, :, r, :, cols] = dq[rows].reshape(SIDE, WIDE, DIM).astype(BF16)
             kp[u, :, :, before] = (kacc[...] + dk[TOK:]).reshape(SIDE, SIDE, WIDE, DIM).astype(BF16)
             vp[u, :, :, before] = (vacc[...] + dv[TOK:]).reshape(SIDE, SIDE, WIDE, DIM).astype(BF16)
             kacc[...] = dk[:TOK]
             vacc[...] = dv[:TOK]
-            for n, (buf, dst) in enumerate(((att_o, att_hbm), (dq_o, dq_hbm))):
-                for k in (1, 3, 2):
-                    b, dev = a_peer(t, k)
-                    remote(
-                        buf.at[u, b, r], dst.at[0, OWN * a + r, :, lanes], out_send.at[n], out_recv.at[n], dev
-                    )
-                local(buf.at[u, a, r], dst.at[0, OWN * a + r, :, lanes], out_recv.at[n])
+            if u < 2:
+                bulk(u, r, 1)
             return 0
 
         lax.fori_loop(0, OWN, one_round, 0)
@@ -259,15 +272,64 @@
             g, dev = g_peer(t, k)
             for n, (src, dst) in enumerate(((kp, kr), (vp, vr))):
                 remote(src.at[u, g], dst.at[u, k - 1], rs_send.at[n], rs_recv.at[u, n], dev)
-        for i in range(SIDE):
-            for j in range(2):
-                gsend[u, i, j : j + 1, :] = jnp.sum(gacc[2 * i + j], axis=0, keepdims=True)
-        for i in range(SIDE):
-            owner = h * SIDE + i
-
-            @pl.when(owner != ctx)
+        for g in range(GROUP):
+            gpart[u, g // 2, g % 2 : g % 2 + 1, :] = jnp.sum(gacc[g], axis=0, keepdims=True)
+        gain_rows(u, True)
+
+    def gain_rows(u, go):
+        t, h = u % 2, UNIT_HEAD[u]
+        if t == 0:
+
+            @pl.when(z != h)
             def _():
-                remote(gsend.at[u, i], grecv.at[(ctx - owner + 15) % 16], g_send, g_recv, at_ctx(owner))
+                copy = pltpu.make_async_remote_copy(
+                    src_ref=gpart.at[u], dst_ref=ghalf.at[u, (z - h + 3) % SIDE], send_sem=gr_send.at[u],
+                    recv_sem=gr_recv.at[u], device_id=at_ctx(h * SIDE + x), device_id_type=MESH,
+                )
+                copy.start() if go else copy.wait_send()
+        elif go:
+            for k in (1, 3, 2):
+                i, dev = g_peer(t, k)
+                remote(gpart.at[u, i], ghalf.at[u, k - 1, 0], gr_send.at[u], gr_recv.at[u], dev)
+        else:
+            drain(gpart.at[u, pl.ds(0, SIDE - 1)], gr_send.at[u])
+
+    def gain_cols(u, go):
+        t, h = u % 2, UNIT_HEAD[u]
+        if t == 0:
+
+            @pl.when(z == h)
+            def _():
+                if go:
+                    drain(ghalf.at[u], gr_recv.at[u])
+                    gsum[u] = gpart[u] + ghalf[u, 0] + ghalf[u, 1] + ghalf[u, 2]
+                    for k in (1, 3, 2):
+                        i, dev = a_peer(t, k)
+                        remote(gsum.at[u, i], gside.at[u, k - 1], ga_send.at[u], ga_recv.at[u], dev)
+                else:
+                    drain(gsum.at[u, pl.ds(0, SIDE - 1)], ga_send.at[u])
+        else:
+            if go:
+                drain(ghalf.at[u, pl.ds(0, SIDE - 1), 0], gr_recv.at[u])
+                gsum[u, x] = gpart[u, x] + ghalf[u, 0, 0] + ghalf[u, 1, 0] + ghalf[u, 2, 0]
+
+            @pl.when(z != h)
+            def _():
+                copy = pltpu.make_async_remote_copy(
+                    src_ref=gsum.at[u, x], dst_ref=gside.at[u, (z - h + 3) % SIDE], send_sem=ga_send.at[u],
+                    recv_sem=ga_recv.at[u], device_id=at_ctx(h * SIDE + x), device_id_type=MESH,
+                )
+                copy.start() if go else copy.wait_send()
+
+    def gain_over_dp(u):
+        h = UNIT_HEAD[u]
+
+        @pl.when(z == h)
+        def _():
+            drain(gside.at[u], ga_recv.at[u])
+            gfin[...] = gsum[u, x] + gside[u, 0] + gside[u, 1] + gside[u, 2]
+            for i in range(1, 8):
+                remote(gfin, gdp.at[i - 1], d_send, d_recv, ((dp + i) % 8, ctx))
 
     def reduce_back(u):
         t = u % 2
@@ -281,6 +343,7 @@
                 b, dev = a_peer(t, k)
                 remote(total.at[u, b], back.at[u, me_a(t)], aa_send.at[n], aa_recv.at[u, n], dev)
             local(total.at[u, me_a(t)], back.at[u, me_a(t)], aa_recv.at[u, n])
+        gain_cols(u, True)
 
     def finish(u):
         h = UNIT_HEAD[u]
@@ -294,30 +357,29 @@
                     val = (val.astype(F32) + back[u, b + 1, 0].astype(F32)).astype(BF16)
                 out[0, rho, :, cols] = val
 
-    gsend[...] = jnp.zeros_like(gsend)
-    for u in range(4):
-        unit(u)
-        if u >= 1:
-            reduce_back(u - 1)
-    drain(grecv.at[pl.ds(0, 15)], g_recv)
-    total = jnp.zeros((8, DIM), F32)
-    for u in range(4):
-        for i in range(SIDE):
-            total += jnp.where(UNIT_HEAD[u] * SIDE + i == ctx, gsend[u, i], 0.0)
-    for i in range(15):
-        total += grecv[i]
-    gsum[...] = total
-    for i in range(1, 8):
-        remote(gsum, gdp.at[i - 1], d_send, d_recv, ((dp + i) % 8, ctx))
+    unit(0)
+    unit(1)
+    reduce_back(0)
+    unit(2)
+    reduce_back(1)
+    unit(3)
+    bulk(2, 0, OWN)
+    bulk(3, 0, OWN // 2)
+    reduce_back(2)
+    for u in range(2):
+        gain_over_dp(u)
     reduce_back(3)
+    bulk(3, OWN // 2, OWN // 2)
+    gain_over_dp(2)
     for u in range(3):
         finish(u)
-    drain(gdp.at[pl.ds(0, 7)], d_recv)
-    total = gsum[...]
+    gain_over_dp(3)
+    finish(3)
+    drain(gdp, d_recv)
+    total = gfin[...]
     for i in range(7):
         total += gdp[i]
-    gg_ref[...] = total[:2] * (1.0 / 128.0)
-    finish(3)
+    gg_ref[...] = total * (1.0 / 128.0)
     for n, buf in enumerate((kin, vin)):
         drain(buf.at[:, 0, pl.ds(0, SIDE - 1)], kv_send.at[n])
         drain(buf.at[:, pl.ds(0, SIDE - 1)], kvg_send.at[n])
@@ -330,12 +392,33 @@
     for n, (buf, dst) in enumerate(((att_o, att_hbm), (dq_o, dq_hbm))):
         drain(buf.at[:, pl.ds(0, SIDE - 1)], out_send.at[n])
         drain(dst, out_recv.at[n])
-    drain(grecv.at[pl.ds(0, 15)], g_send)
-    drain(gdp.at[pl.ds(0, 7)], d_send)
+    for u in range(4):
+        gain_rows(u, False)
+        gain_cols(u, False)
+    drain(gdp, d_send)
+
+
+def write_out(att, dq, dk, dv, gg, att_out, dq_out, dk_out, dv_out, gg_out, big, small):
+    copies = []
+    for n, (src, dst) in enumerate(((att, att_out), (dq, dq_out))):
+        for i in range(4):
+            part = pl.ds(i * 4, 4)
+            copies.append(pltpu.make_async_copy(src.at[:, part], dst.at[:, part], big.at[n, i]))
+    for n, (src, dst) in enumerate(((dk, dk_out), (dv, dv_out))):
+        copies.append(pltpu.make_async_copy(src, dst, small.at[n]))
+    for copy in copies:
+        copy.start()
+    for i in range(2):
+        gg_out[pl.ds(i * DIM, DIM)] = gg[i]
+    for copy in copies:
+        copy.wait()
 
 
 def body(queries, key_rows, values, out_grad, out_gain, documents):
-    gain = out_gain.reshape(HEADS * GROUP, DIM).astype(F32)
+    queries, key_rows, values, out_grad, out_gain, documents = (
+        pltpu.with_memory_space_constraint(a, pltpu.HBM)
+        for a in (queries, key_rows, values, out_grad, out_gain, documents)
+    )
     any_spec = pl.BlockSpec(memory_space=pl.ANY)
     vmem = pl.BlockSpec(memory_space=pltpu.VMEM)
     wide = pltpu.VMEM((4, SIDE, OWN, WIDE, GROUP * DIM), BF16)
@@ -352,28 +435,47 @@
             jax.ShapeDtypeStruct(key_rows.shape, BF16),
             jax.ShapeDtypeStruct((2, DIM), F32),
         ),
-        in_specs=[any_spec, any_spec, any_spec, any_spec, vmem, vmem],
+        in_specs=[any_spec] * 6,
         out_specs=(any_spec, any_spec, vmem, vmem, vmem),
         scratch_shapes=[
             wide, wide, narrow, narrow, wide, wide, narrow, narrow, narrow3, narrow3, flat, flat, flat, flat,
+            pltpu.VMEM(out_gain.shape, BF16),
+            pltpu.VMEM(documents.shape, jnp.int32),
             pltpu.VMEM((2, TOK, ROWS), F32),
             pltpu.VMEM((2, OWN, TOK, ROWS), F32),
             pltpu.VMEM((TOK, DIM), F32),
             pltpu.VMEM((TOK, DIM), F32),
             pltpu.VMEM((GROUP, WIDE, DIM), F32),
-            pltpu.VMEM((4, SIDE, 8, DIM), F32),
-            pltpu.VMEM((15, 8, DIM), F32),
-            pltpu.VMEM((8, DIM), F32),
-            pltpu.VMEM((7, 8, DIM), F32),
+            pltpu.VMEM((HEADS * GROUP, DIM), F32),
+            pltpu.VMEM((4, SIDE, 2, DIM), F32),
+            pltpu.VMEM((4, SIDE - 1, SIDE, 2, DIM), F32),
+            pltpu.VMEM((4, SIDE, 2, DIM), F32),
+            pltpu.VMEM((4, SIDE - 1, 2, DIM), F32),
+            pltpu.VMEM((2, DIM), F32),
+            pltpu.VMEM((7, 2, DIM), F32),
             dma((2,)), dma((4, 2)), dma((2,)), dma((4, 2)), dma((2,)), dma((4, 2)), dma((2,)), dma((2,)),
-            dma((2,)), dma((4, 2)), dma((2,)), dma((4, 2)), dma, dma, dma, dma,
+            dma((2,)), dma((4, 2)), dma((2,)), dma((4, 2)), dma((4,)), dma((4,)), dma((4,)), dma((4,)), dma, dma, dma((2,)),
         ],
         compiler_params=pltpu.CompilerParams(
             collective_id=0, has_side_effects=True, vmem_limit_bytes=48 * 1024 * 1024
         ),
         name="packed_attention",
-    )(queries, key_rows, values, out_grad, gain, documents)
-    return att, dq, dk, dv, gg.reshape(2 * DIM)
+    )(queries, key_rows, values, out_grad, out_gain, documents)
+    return pl.pallas_call(
+        write_out,
+        out_shape=(
+            jax.ShapeDtypeStruct(queries.shape, BF16),
+            jax.ShapeDtypeStruct(queries.shape, BF16),
+            jax.ShapeDtypeStruct(key_rows.shape, BF16),
+            jax.ShapeDtypeStruct(key_rows.shape, BF16),
+            jax.ShapeDtypeStruct((2 * DIM,), F32),
+        ),
+        in_specs=[any_spec] * 4 + [vmem],
+        out_specs=(any_spec, any_spec, any_spec, any_spec, vmem),
+        scratch_shapes=[dma((2, 4)), dma((2,))],
+        compiler_params=pltpu.CompilerParams(vmem_limit_bytes=1024 * 1024),
+        name="write_out",
+    )(att, dq, dk, dv, gg)
 
 
 def solution(mesh):

time: 63.8 us -> 58.2 us (0.912); the launches traced: 63.5 us -> 57 us
  local copies, waits for them, and re-layouts: 8.07 us -> 0 us
  Pallas kernels: 54.1 us -> 56.4 us
  other arithmetic: 0.71 us -> 0 us
    unnamed x15 -> x0, local copies, waits for them, and re-layouts: 8.07 us -> none
    pallas_call x0 -> x1, Pallas kernels: none -> 2.04 us  [body(): pl.pallas_call(write_out, out_shape=(jax.ShapeDtypeStruct(queries.shape,...]
    convert_element_type x1 -> x0, other arithmetic: 0.71 us -> none  [body(): gain = out_gain.reshape(HEADS * GROUP, DIM).astype(F32)]
where the time goes in v2:
time: 58.2 us; the launch traced here: 57 us
  Pallas kernels  56.4 us (97%)
  between operations  0.64 us (1%)
    pallas_call x1, Pallas kernels, body(): pl.pallas_call(kernel, out_shape=(jax.ShapeDtypeStruct(queries.shape, BF1...  54.4 us
    pallas_call x1, Pallas kernels, body(): pl.pallas_call(write_out, out_shape=(jax.ShapeDtypeStruct(queries.shape,...  2.04 us

profile of v2, /device:TPU:0, one launch (start us, length us, event | category | flops | bytes accessed | tf_op | source)
XLA Modules:
  0.0 57.0 jit_solution(10048016513771833189)
XLA Ops:
  0.6 54.4 %packed_attention.1 = (bf16[1,16,8,4096]{3,2,1,0:T(8,128)(2,1)S(1)}, bf16[1,16,8,4096]{3,2,1,0:T(8,128)(2,1)S(1)}, bf16[1,16,8,512]{3,2,1,0:T(8,128)(2,1)S(1)}, ...) custom-call(bf16[1,16,8,4096]{3,2,1,0:T(8,128)(2,1)} %q_hbm.1, bf16[1,16,8,512]{3,2,1,0:T(8,128)(2,1)} %k_hbm.1, ...), custom_call_target="tpu_custom_call" | custom-call | tf_op jit(solution)/shard_map/packed_attention/pallas_call | solution.py:429
  55.0 2.0 %write_out.1 = (bf16[1,16,8,4096]{3,2,1,0:T(8,128)(2,1)}, bf16[1,16,8,4096]{3,2,1,0:T(8,128)(2,1)}, bf16[1,16,8,512]{3,2,1,0:T(8,128)(2,1)}, bf16[1,16,8,512]{3,2,1,0:T(8,128)(2,1)}, f32[256]{0:T(256)}) custom-call(bf16[1,16,8,4096]{3,2,1,0:T(8,128)(2,1)S(1)} %get-tuple-element.10.att, bf16[1,16,8,4096]{3,2,1,0:T(8,128)(2,1)S(1)} %get-tuple-element.11.dq, ...), custom_call_target="tpu_custom_call" | custom-call | tf_op jit(solution)/shard_map/write_out/pallas_call | solution.py:464

commit v3 on v2

--- a/solution.py
+++ b/solution.py
@@ -43,7 +43,7 @@
     qin, gin, kin, vin, att_o, dq_o, kp, vp, kr, vr, ks, vs, ka, va,
     gain_ref, docs_ref, le_ref, bias_ref, kacc, vacc, gacc, gains, gpart, ghalf, gsum, gside, gfin, gdp,
     kv_send, kv_recv, kvg_send, kvg_recv, q_send, q_recv, out_send, out_recv,
-    rs_send, rs_recv, aa_send, aa_recv, gr_send, gr_recv, ga_send, ga_recv, d_send, d_recv, small,
+    rs_send, rs_recv, aa_send, aa_recv, gr_send, gr_recv, ga_send, ga_recv, d_send, d_recv, small, hello,
 ):
     dp = lax.axis_index("dp")
     ctx = lax.axis_index("ctx")
@@ -87,7 +87,11 @@
         for k in range(1, SIDE):
             pl.semaphore_signal(barrier, inc=1, device_id=a_peer(t, k)[1], device_id_type=MESH)
     for i in range(1, 8):
-        pl.semaphore_signal(barrier, inc=1, device_id=((dp + i) % 8, ctx), device_id_type=MESH)
+
+        @pl.when(dp + i < 8)
+        def _():
+            pl.semaphore_signal(barrier, inc=1, device_id=(dp + i, ctx), device_id_type=MESH)
+
 
     def kv_local(u):
         t, h = u % 2, UNIT_HEAD[u]
@@ -103,51 +107,72 @@
         for n, (src, dst) in enumerate(((q_hbm, qin), (g_hbm, gin))):
             local(src.at[0, pl.ds(OWN * a, OWN), :, lanes], dst.at[u, a], q_recv.at[u, n])
 
-    def kv_first(u):
-        t, h = u % 2, UNIT_HEAD[u]
-        lanes = pl.ds(h * DIM, DIM)
+    def kv_first(pair):
         for k in (1, 3, 2):
-            a, dev = a_peer(t, k)
             for n, (src, dst) in enumerate(((k_hbm, kin), (v_hbm, vin))):
+                for u in pair:
+                    t, h = u % 2, UNIT_HEAD[u]
+                    a, dev = a_peer(t, k)
+                    remote(
+                        src.at[0, pl.ds(OWN * a - off(a), SLOTS), :, pl.ds(h * DIM, DIM)],
+                        dst.at[u, me_g(t), me_a(t)], kv_send.at[n], kv_recv.at[u, n], dev,
+                    )
+
+    def kv_near(pair):
+        for u in pair:
+            for n, buf in enumerate((kin, vin)):
+                drain(buf.at[u, 0], kv_recv.at[u, n])
+        for k in (1, 3):
+            for n, buf in enumerate((kin, vin)):
+                for u in pair:
+                    t = u % 2
+                    _, dev = g_peer(t, k)
+                    remote(buf.at[u, me_g(t)], buf.at[u, me_g(t)], kvg_send.at[n], kvg_recv.at[u, n, k - 1], dev)
+
+    def kv_far(pair):
+        for n, (buf, k) in enumerate(((kin, 1), (vin, 3))):
+            for u in pair:
+                t = u % 2
+                drain(buf.at[u, 0], kvg_recv.at[u, n, k - 1])
+                origin = (me_g(t) + SIDE - k) % SIDE
+                _, dev = g_peer(t, k)
+                remote(buf.at[u, origin], buf.at[u, origin], kvg_send.at[n], kvg_recv.at[u, n, 1], dev)
+
+    def q_out(pair, n):
+        src, dst = ((q_hbm, qin), (g_hbm, gin))[n]
+        for k in (1, 3, 2):
+            for u in pair:
+                t, h = u % 2, UNIT_HEAD[u]
+                a, dev = a_peer(t, k)
                 remote(
-                    src.at[0, pl.ds(OWN * a - off(a), SLOTS), :, lanes], dst.at[u, me_g(t), me_a(t)],
-                    kv_send.at[n], kv_recv.at[u, n], dev,
+                    src.at[0, pl.ds(OWN * a, OWN), :, pl.ds(h * GROUP * DIM, GROUP * DIM)],
+                    dst.at[u, me_a(t)], q_send.at[n], q_recv.at[u, n], dev,
                 )
 
-    def kv_gather(u):
-        t = u % 2
-        for n, buf in enumerate((kin, vin)):
-            drain(buf.at[u, 0], kv_recv.at[u, n])
-        for k in (1, 3, 2):
-            _, dev = g_peer(t, k)
-            for n, buf in enumerate((kin, vin)):
-                remote(buf.at[u, me_g(t)], buf.at[u, me_g(t)], kvg_send.at[n], kvg_recv.at[u, n], dev)
-
-    def q_send_all(u):
-        t, h = u % 2, UNIT_HEAD[u]
-        lanes = pl.ds(h * GROUP * DIM, GROUP * DIM)
-        for k in (1, 3, 2):
-            a, dev = a_peer(t, k)
-            for n, (src, dst) in enumerate(((q_hbm, qin), (g_hbm, gin))):
-                remote(
-                    src.at[0, pl.ds(OWN * a, OWN), :, lanes], dst.at[u, me_a(t)], q_send.at[n], q_recv.at[u, n], dev
-                )
-
+    first, second = (0, 1), (2, 3)
     local(gain_hbm, gain_ref, small.at[0])
     local(docs_hbm, docs_ref, small.at[1])
     for u in range(4):
         kv_local(u)
     for u in range(4):
         q_local(u)
-    pl.semaphore_wait(barrier, 13)
-    for u in range(4):
-        kv_first(u)
-    for u in (0, 1):
-        q_send_all(u)
-    for u in range(4):
-        kv_gather(u)
-    for u in (2, 3):
-        q_send_all(u)
+    pl.semaphore_wait(barrier, 6 + dp)
+    for i in range(1, 8):
+
+        @pl.when(dp >= i)
+        def _():
+            pl.semaphore_signal(hello, inc=1, device_id=(dp - i, ctx), device_id_type=MESH)
+
+    kv_first(first)
+    kv_first(second)
+    q_out(first, 0)
+    kv_near(first)
+    kv_near(second)
+    q_out(first, 1)
+    kv_far(first)
+    q_out(second, 0)
+    kv_far(second)
+    q_out(second, 1)
 
     drain(gain_ref, small.at[0])
     drain(docs_ref, small.at[1])
@@ -191,30 +216,33 @@
 
         lax.fori_loop(0, OWN, one_bias, 0)
 
-    def bulk(u, r, count):
-        t, h = u % 2, UNIT_HEAD[u]
-        a = me_a(t)
-        lanes = pl.ds(h * GROUP * DIM, GROUP * DIM)
-        rounds = pl.ds(r, count)
+    def bulk(pair, r, count):
         for n, (buf, dst) in enumerate(((att_o, att_hbm), (dq_o, dq_hbm))):
-            there = dst.at[0, pl.ds(OWN * a + r, count), :, lanes]
-            for k in (1, 3, 2):
-                b, dev = a_peer(t, k)
-                remote(buf.at[u, b, rounds], there, out_send.at[n], out_recv.at[n], dev)
-            local(buf.at[u, a, rounds], there, out_recv.at[n])
-
-    def unit(u):
-        t, h = u % 2, UNIT_HEAD[u]
-        a = me_a(t)
-        for n, buf in enumerate((qin, gin)):
-            drain(buf.at[u], q_recv.at[u, n])
-        for n, buf in enumerate((kin, vin)):
-            drain(buf.at[u, pl.ds(0, SIDE - 1)], kvg_recv.at[u, n])
+            for k in (1, 3, 2, 0):
+                for u in pair:
+                    t, h = u % 2, UNIT_HEAD[u]
+                    there = dst.at[0, pl.ds(OWN * me_a(t) + r, count), :, pl.ds(h * GROUP * DIM, GROUP * DIM)]
+                    b, dev = a_peer(t, k)
+                    here = buf.at[u, b, pl.ds(r, count)]
+                    if k:
+                        remote(here, there, out_send.at[n], out_recv.at[n], dev)
+                    else:
+                        local(here, there, out_recv.at[n])
+
+    def compute(pair, spread):
+        for u in pair:
+            for n, buf in enumerate((qin, gin)):
+                drain(buf.at[u], q_recv.at[u, n])
+            for n, (buf, rest) in enumerate(((kin, (2, 3)), (vin, (1, 2)))):
+                for k in rest:
+                    drain(buf.at[u, 0], kvg_recv.at[u, n, k - 1])
         kacc[...] = jnp.zeros_like(kacc)
         vacc[...] = jnp.zeros_like(vacc)
         gacc[...] = jnp.zeros_like(gacc)
 
-        def one_round(r, _):
+        def one_round(u, r):
+            t, h = u % 2, UNIT_HEAD[u]
+            a = me_a(t)
             here = r + off(a)
             before = (here + SLOTS - 1) % SLOTS
 
@@ -253,28 +281,50 @@
                 rows = slice(g * SIDE * WIDE, (g + 1) * SIDE * WIDE)
                 cols = slice(g * DIM, (g + 1) * DIM)
                 a_g = attn[rows].reshape(SIDE, WIDE, DIM)
-                gacc[g] += jnp.sum(a_g * gin[u, :, r, :, cols].astype(F32), axis=0)
+                gacc[t, g] += jnp.sum(a_g * gin[u, :, r, :, cols].astype(F32), axis=0)
                 att_o[u, :, r, :, cols] = (a_g * gains[h * GROUP + g : h * GROUP + g + 1, :]).astype(BF16)
                 dq_o[u, :, r, :, cols] = dq[rows].reshape(SIDE, WIDE, DIM).astype(BF16)
-            kp[u, :, :, before] = (kacc[...] + dk[TOK:]).reshape(SIDE, SIDE, WIDE, DIM).astype(BF16)
-            vp[u, :, :, before] = (vacc[...] + dv[TOK:]).reshape(SIDE, SIDE, WIDE, DIM).astype(BF16)
-            kacc[...] = dk[:TOK]
-            vacc[...] = dv[:TOK]
-            if u < 2:
-                bulk(u, r, 1)
+            kp[u, :, :, before] = (kacc[t] + dk[TOK:]).reshape(SIDE, SIDE, WIDE, DIM).astype(BF16)
+            vp[u, :, :, before] = (vacc[t] + dv[TOK:]).reshape(SIDE, SIDE, WIDE, DIM).astype(BF16)
+            kacc[t] = dk[:TOK]
+            vacc[t] = dv[:TOK]
+
+        def both(r, _):
+            for u in pair:
+                one_round(u, r)
+            if spread:
+                bulk(pair, r, 1)
             return 0
 
-        lax.fori_loop(0, OWN, one_round, 0)
-        last = OWN - 1 + off(a)
-        kp[u, :, :, last] = kacc[...].reshape(SIDE, SIDE, WIDE, DIM).astype(BF16)
-        vp[u, :, :, last] = vacc[...].reshape(SIDE, SIDE, WIDE, DIM).astype(BF16)
-        for k in (1, 3, 2):
-            g, dev = g_peer(t, k)
-            for n, (src, dst) in enumerate(((kp, kr), (vp, vr))):
-                remote(src.at[u, g], dst.at[u, k - 1], rs_send.at[n], rs_recv.at[u, n], dev)
-        for g in range(GROUP):
-            gpart[u, g // 2, g % 2 : g % 2 + 1, :] = jnp.sum(gacc[g], axis=0, keepdims=True)
-        gain_rows(u, True)
+        lax.fori_loop(0, OWN, both, 0)
+        for u in pair:
+            t = u % 2
+            last = OWN - 1 + off(me_a(t))
+            kp[u, :, :, last] = kacc[t].reshape(SIDE, SIDE, WIDE, DIM).astype(BF16)
+            vp[u, :, :, last] = vacc[t].reshape(SIDE, SIDE, WIDE, DIM).astype(BF16)
+            for g in range(GROUP):
+                gpart[u, g // 2, g % 2 : g % 2 + 1, :] = jnp.sum(gacc[t, g], axis=0, keepdims=True)
+
+    def sums_near(pair):
+        for n, (part, got, k) in enumerate(((kp, kr, 3), (vp, vr, 1))):
+            for u in pair:
+                t = u % 2
+                _, dev = g_peer(t, SIDE - k)
+                remote(part.at[u, (me_g(t) + 2) % SIDE], got.at[u, 1], rs_send.at[n], rs_recv.at[u, n, 1], dev)
+        for n, (part, got, k) in enumerate(((kp, kr, 3), (vp, vr, 1))):
+            for u in pair:
+                g, dev = g_peer(u % 2, k)
+                remote(part.at[u, g], got.at[u, 0], rs_send.at[n], rs_recv.at[u, n, 0], dev)
+        for u in pair:
+            gain_rows(u, True)
+
+    def sums_far(pair):
+        for n, (part, got, k) in enumerate(((kp, kr, 1), (vp, vr, 3))):
+            for u in pair:
+                g, dev = g_peer(u % 2, k)
+                drain(got.at[u, 1], rs_recv.at[u, n, 1])
+                got[u, 1] = (got[u, 1].astype(F32) + part[u, g].astype(F32)).astype(BF16)
+                remote(got.at[u, 1], got.at[u, 2], rs_send.at[n], rs_recv.at[u, n, 2], dev)
 
     def gain_rows(u, go):
         t, h = u % 2, UNIT_HEAD[u]
@@ -331,19 +381,22 @@
             for i in range(1, 8):
                 remote(gfin, gdp.at[i - 1], d_send, d_recv, ((dp + i) % 8, ctx))
 
-    def reduce_back(u):
-        t = u % 2
+    def sums_back(pair):
         for n, (part, got, total, back) in enumerate(((kp, kr, ks, ka), (vp, vr, vs, va))):
-            drain(got.at[u], rs_recv.at[u, n])
-            acc = part[u, me_g(t)].astype(F32)
-            for k in range(SIDE - 1):
-                acc += got[u, k].astype(F32)
-            total[u] = acc.astype(BF16)
+            for u in pair:
+                drain(got.at[u, 0], rs_recv.at[u, n, 0])
+                drain(got.at[u, 2], rs_recv.at[u, n, 2])
+                total[u] = (
+                    part[u, me_g(u % 2)].astype(F32) + got[u, 0].astype(F32) + got[u, 2].astype(F32)
+                ).astype(BF16)
             for k in (1, 3, 2):
-                b, dev = a_peer(t, k)
-                remote(total.at[u, b], back.at[u, me_a(t)], aa_send.at[n], aa_recv.at[u, n], dev)
-            local(total.at[u, me_a(t)], back.at[u, me_a(t)], aa_recv.at[u, n])
-        gain_cols(u, True)
+                for u in pair:
+                    t = u % 2
+                    b, dev = a_peer(t, k)
+                    remote(total.at[u, b], back.at[u, me_a(t)], aa_send.at[n], aa_recv.at[u, n], dev)
+            for u in pair:
+                a = me_a(u % 2)
+                local(total.at[u, a], back.at[u, a], aa_recv.at[u, n])
 
     def finish(u):
         h = UNIT_HEAD[u]
@@ -357,24 +410,33 @@
                     val = (val.astype(F32) + back[u, b + 1, 0].astype(F32)).astype(BF16)
                 out[0, rho, :, cols] = val
 
-    unit(0)
-    unit(1)
-    reduce_back(0)
-    unit(2)
-    reduce_back(1)
-    unit(3)
-    bulk(2, 0, OWN)
-    bulk(3, 0, OWN // 2)
-    reduce_back(2)
-    for u in range(2):
+    compute(first, False)
+    sums_near(first)
+    bulk(first, 0, 4)
+    compute(second, False)
+    sums_near(second)
+    sums_far(first)
+    for u in first:
+        gain_cols(u, True)
+    bulk(second, 0, 1)
+    sums_far(second)
+    for u in second:
+        gain_cols(u, True)
+    sums_back(first)
+
+    @pl.when(dp < 7)
+    def _():
+        pl.semaphore_wait(hello, 7 - dp)
+
+    for u in first:
         gain_over_dp(u)
-    reduce_back(3)
-    bulk(3, OWN // 2, OWN // 2)
-    gain_over_dp(2)
-    for u in range(3):
+    bulk(second, 1, 1)
+    sums_back(second)
+    for u in second:
+        gain_over_dp(u)
+    bulk(second, 2, 2)
+    for u in range(4):
         finish(u)
-    gain_over_dp(3)
-    finish(3)
     drain(gdp, d_recv)
     total = gfin[...]
     for i in range(7):
@@ -443,9 +505,9 @@
             pltpu.VMEM(documents.shape, jnp.int32),
             pltpu.VMEM((2, TOK, ROWS), F32),
             pltpu.VMEM((2, OWN, TOK, ROWS), F32),
-            pltpu.VMEM((TOK, DIM), F32),
-            pltpu.VMEM((TOK, DIM), F32),
-            pltpu.VMEM((GROUP, WIDE, DIM), F32),
+            pltpu.VMEM((2, TOK, DIM), F32),
+            pltpu.VMEM((2, TOK, DIM), F32),
+            pltpu.VMEM((2, GROUP, WIDE, DIM), F32),
             pltpu.VMEM((HEADS * GROUP, DIM), F32),
             pltpu.VMEM((4, SIDE, 2, DIM), F32),
             pltpu.VMEM((4, SIDE - 1, SIDE, 2, DIM), F32),
@@ -453,8 +515,8 @@
             pltpu.VMEM((4, SIDE - 1, 2, DIM), F32),
             pltpu.VMEM((2, DIM), F32),
             pltpu.VMEM((7, 2, DIM), F32),
-            dma((2,)), dma((4, 2)), dma((2,)), dma((4, 2)), dma((2,)), dma((4, 2)), dma((2,)), dma((2,)),
-            dma((2,)), dma((4, 2)), dma((2,)), dma((4, 2)), dma((4,)), dma((4,)), dma((4,)), dma((4,)), dma, dma, dma((2,)),
+            dma((2,)), dma((4, 2)), dma((2,)), dma((4, 2, 3)), dma((2,)), dma((4, 2)), dma((2,)), dma((2,)),
+            dma((2,)), dma((4, 2, 3)), dma((2,)), dma((4, 2)), dma((4,)), dma((4,)), dma((4,)), dma((4,)), dma, dma, dma((2,)), pltpu.SemaphoreType.REGULAR,
         ],
         compiler_params=pltpu.CompilerParams(
             collective_id=0, has_side_effects=True, vmem_limit_bytes=48 * 1024 * 1024

time: 58.2 us -> 49.4 us (0.85); the launches traced: 57 us -> 49.3 us
  Pallas kernels: 56.4 us -> 48.6 us
    pallas_call x1, Pallas kernels: 54.4 us -> 46.6 us  [body(): pl.pallas_call(kernel, out_shape=(jax.ShapeDtypeStruct(queries.shape, BF1...]
where the time goes in v3:
time: 49.4 us; the launch traced here: 49.3 us
  Pallas kernels  48.6 us (98%)
  between operations  0.64 us (1%)
    pallas_call x1, Pallas kernels, body(): pl.pallas_call(kernel, out_shape=(jax.ShapeDtypeStruct(queries.shape, BF1...  46.6 us
    pallas_call x1, Pallas kernels, body(): pl.pallas_call(write_out, out_shape=(jax.ShapeDtypeStruct(queries.shape,...  2.04 us

profile of v3, /device:TPU:0, one launch (start us, length us, event | category | flops | bytes accessed | tf_op | source)
XLA Modules:
  0.0 49.3 jit_solution(12602325276231217321)
XLA Ops:
  0.6 46.6 %packed_attention.1 = (bf16[1,16,8,4096]{3,2,1,0:T(8,128)(2,1)S(1)}, bf16[1,16,8,4096]{3,2,1,0:T(8,128)(2,1)S(1)}, bf16[1,16,8,512]{3,2,1,0:T(8,128)(2,1)S(1)}, ...) custom-call(bf16[1,16,8,4096]{3,2,1,0:T(8,128)(2,1)} %q_hbm.1, bf16[1,16,8,512]{3,2,1,0:T(8,128)(2,1)} %k_hbm.1, ...), custom_call_target="tpu_custom_call" | custom-call | tf_op jit(solution)/shard_map/packed_attention/pallas_call | solution.py:491
  47.2 2.0 %write_out.1 = (bf16[1,16,8,4096]{3,2,1,0:T(8,128)(2,1)}, bf16[1,16,8,4096]{3,2,1,0:T(8,128)(2,1)}, bf16[1,16,8,512]{3,2,1,0:T(8,128)(2,1)}, bf16[1,16,8,512]{3,2,1,0:T(8,128)(2,1)}, f32[256]{0:T(256)}) custom-call(bf16[1,16,8,4096]{3,2,1,0:T(8,128)(2,1)S(1)} %get-tuple-element.10.att, bf16[1,16,8,4096]{3,2,1,0:T(8,128)(2,1)S(1)} %get-tuple-element.11.dq, ...), custom_call_target="tpu_custom_call" | custom-call | tf_op jit(solution)/shard_map/write_out/pallas_call | solution.py:526

commit v4 on v3

v4 whole, which is shorter than its diff:
```python
import functools
import math

import jax
import jax.numpy as jnp
from jax import lax
from jax.experimental import pallas as pl
from jax.experimental.pallas import tpu as pltpu
from jax.sharding import PartitionSpec as P

MESH = pl.DeviceIdType.MESH
F32 = jnp.float32
BF16 = jnp.bfloat16
SIDE = 4
ROUNDS = 16
PART = ROUNDS // SIDE
SLOTS = 2 * PART + 1
WIDE = 8
DIM = 128
GROUP = 8
HEADS = 4
TOK = 128
ROWS = SIDE * WIDE * GROUP
NEG_BIG = -1e30
IN_SLOTS = ((0, 4), (0, 5), (4, 4), (5, 4))
OUT_SLOTS = ((0, 3), (0, 4), (3, 5), (4, 5))


def dot_t(a, b):
    return lax.dot_general(a, b, (((1,), (1,)), ((), ())), preferred_element_type=F32)


def dot_tn(a, b):
    return lax.dot_general(a, b, (((0,), (0,)), ((), ())), preferred_element_type=F32)


def dot_n(a, b):
    return lax.dot_general(a, b, (((1,), (0,)), ((), ())), preferred_element_type=F32)


def kernel(
    q_hbm, k_hbm, v_hbm, g_hbm, gain_hbm, docs_hbm,
    att_hbm, dq_hbm, dk_ref, dv_ref, gg_ref,
    qin, gin, kin, vin, att_o, dq_o, kp, vp, kr, vr, ks, vs, ka, va,
    kst, gain_ref, docs_ref, le_ref, bias_ref, kacc, vacc, gacc, gains, gpart, ghalf, gsum, gside, gdiag, gfin, gdp,
    kv_send, kv_recv, kvg_send, kvg_recv, q_send, q_recv, out_send, out_recv,
    rs_send, rs_recv, aa_send, aa_recv, gr_send, gr_recv, ga_send, ga_recv, d_send, d_recv, small, hello, kst_sem,
):
    dp = lax.axis_index("dp")
    ctx = lax.axis_index("ctx")
    z = ctx // SIDE
    x = ctx % SIDE
    scale = 1.0 / math.sqrt(DIM)

    def at_ctx(c):
        return (dp, c)

    def a_peer(t, k):
        a = ((x if t == 0 else z) + k) % SIDE
        return a, at_ctx(z * SIDE + a if t == 0 else a * SIDE + x)

    def g_peer(t, k):
        g = ((z if t == 0 else x) + k) % SIDE
        return g, at_ctx(g * SIDE + x if t == 0 else z * SIDE + g)

    def me_a(t):
        return x if t == 0 else z

    def me_g(t):
        return z if t == 0 else x

    def first_round(u):
        return 2 * PART * (u % 2) + PART * (u // 2)

    def lanes_of(h, width):
        return pl.ds(pl.multiple_of(h * width, width), width)

    def remote(src, dst, ssem, rsem, dev):
        pltpu.make_async_remote_copy(
            src_ref=src, dst_ref=dst, send_sem=ssem, recv_sem=rsem, device_id=dev, device_id_type=MESH
        ).start()

    def local(src, dst, sem):
        pltpu.make_async_copy(src, dst, sem).start()

    def drain(ref, sem):
        pltpu.make_async_copy(ref, ref, sem).wait()

    barrier = pltpu.get_barrier_semaphore()
    for t in range(2):
        for k in range(1, SIDE):
            pl.semaphore_signal(barrier, inc=1, device_id=a_peer(t, k)[1], device_id_type=MESH)
    for i in range(1, 8):

        @pl.when(dp + i < 8)
        def _():
            pl.semaphore_signal(barrier, inc=1, device_id=(dp + i, ctx), device_id_type=MESH)


    def key_rounds(u):
        start, count = IN_SLOTS[u]
        return pl.ds(start + (2 * PART - 1) * (u % 2), count), pl.ds(start, count)

    def kv_local(u):
        t = u % 2
        a = me_a(t)
        rounds, slots = key_rounds(u)
        for n, (src, dst) in enumerate(((k_hbm, kin), (v_hbm, vin))):
            local(src.at[0, rounds, :, lanes_of(a, DIM)], dst.at[t, me_g(t), a, slots], kv_recv.at[u, n])

    def q_local(u):
        a = me_a(u % 2)
        for n, (src, dst) in enumerate(((q_hbm, qin), (g_hbm, gin))):
            local(
                src.at[0, pl.ds(first_round(u), PART), :, lanes_of(a, GROUP * DIM)], dst.at[u, a], q_recv.at[u, n]
            )

    def kv_first(pair):
        for k in (1, 3, 2):
            for n, dst in enumerate((kin, vin)):
                for u in pair:
                    t = u % 2
                    rounds, slots = key_rounds(u)
                    a, dev = a_peer(t, k)
                    remote(
                        kst.at[n, a, rounds], dst.at[t, me_g(t), me_a(t), slots], kv_send.at[u, n], kv_recv.at[u, n], dev
                    )

    def kv_near(pair):
        for u in pair:
            slots = key_rounds(u)[1]
            for n, buf in enumerate((kin, vin)):
                drain(buf.at[u % 2, 0, :, slots], kv_recv.at[u, n])
        for k in (1, 3):
            for n, buf in enumerate((kin, vin)):
                for u in pair:
                    t = u % 2
                    block = buf.at[t, me_g(t), :, key_rounds(u)[1]]
                    remote(block, block, kvg_send.at[u, n], kvg_recv.at[u, n, k - 1], g_peer(t, k)[1])

    def kv_far(pair):
        for n, (buf, k) in enumerate(((kin, 1), (vin, 3))):
            for u in pair:
                t = u % 2
                slots = key_rounds(u)[1]
                drain(buf.at[t, 0, :, slots], kvg_recv.at[u, n, k - 1])
                block = buf.at[t, (me_g(t) + SIDE - k) % SIDE, :, slots]
                remote(block, block, kvg_send.at[u, n], kvg_recv.at[u, n, 1], g_peer(t, k)[1])

    def q_out(pair, n):
        src, dst = ((q_hbm, qin), (g_hbm, gin))[n]
        for k in (1, 3, 2):
            for u in pair:
                t = u % 2
                a, dev = a_peer(t, k)
                remote(
                    src.at[0, pl.ds(first_round(u), PART), :, lanes_of(a, GROUP * DIM)],
                    dst.at[u, me_a(t)], q_send.at[n], q_recv.at[u, n], dev,
                )

    first, second = (0, 1), (2, 3)
    for h in range(HEADS):
        for n, src in enumerate((k_hbm, v_hbm)):
            local(src.at[0, :, :, pl.ds(h * DIM, DIM)], kst.at[n, h], kst_sem)
    pl.semaphore_wait(barrier, 6 + dp)
    drain(kst, kst_sem)
    kv_first(first)
    kv_first(second)
    q_out(first, 0)
    for i in range(1, 8):

        @pl.when(dp >= i)
        def _():
            pl.semaphore_signal(hello, inc=1, device_id=(dp - i, ctx), device_id_type=MESH)

    local(gain_hbm, gain_ref, small.at[0])
    local(docs_hbm, docs_ref, small.at[1])
    for u in range(4):
        kv_local(u)
    for u in range(4):
        q_local(u)
    kv_near(first)
    kv_near(second)
    q_out(first, 1)
    kv_far(first)
    q_out(second, 0)
    kv_far(second)
    q_out(second, 1)

    drain(gain_ref, small.at[0])
    drain(docs_ref, small.at[1])
    for i in range(HEADS * GROUP):
        gains[i : i + 1, :] = gain_ref[pl.ds(i * DIM, DIM)].astype(F32).reshape(1, DIM)
    key_i = lax.broadcasted_iota(jnp.int32, (TOK, ROWS), 0)
    row_i = lax.broadcasted_iota(jnp.int32, (TOK, ROWS), 1) & (SIDE * WIDE - 1)
    for t in range(2):
        def key_col(i):
            return i if t == 0 else ((i >> 3) & 3) * 32 + (i >> 5) * 8 + (i & 7)

        def row_col(i):
            i = i & (SIDE * WIDE - 1)
            return z * 32 + i if t == 0 else (i >> 3) * 32 + x * 8 + (i & 7)

        le = key_col(key_i) <= row_col(row_i)
        le_ref[t] = jnp.where(le, 1.0, 0.0)
        perm = jnp.where(
            key_col(lax.broadcasted_iota(jnp.int32, (TOK, TOK), 0)) == lax.broadcasted_iota(jnp.int32, (TOK, TOK), 1),
            1.0, 0.0,
        ).astype(BF16)
        sel = jnp.where(
            row_col(lax.broadcasted_iota(jnp.int32, (ROWS, TOK), 0)) == lax.broadcasted_iota(jnp.int32, (ROWS, TOK), 1),
            1.0, 0.0,
        ).astype(BF16)

        def doc_row(r):
            return docs_ref[0:1, pl.ds(pl.multiple_of(r * TOK, TOK), TOK)].astype(F32)

        def one_bias(r, _):
            rho = 2 * PART * t + r
            cur = doc_row(rho)
            prev = doc_row((rho + ROUNDS - 1) % ROUNDS)
            k_cur = dot_t(perm, jnp.broadcast_to(cur, (ROWS, TOK)).astype(BF16))
            k_prev = dot_t(perm, jnp.broadcast_to(prev, (ROWS, TOK)).astype(BF16))
            q_doc = dot_t(jnp.broadcast_to(cur, (TOK, TOK)).astype(BF16), sel)
            k_prev = jnp.where(rho > 0, k_prev, -1.0)
            mine = jnp.where(le_ref[t] > 0.5, k_cur, k_prev)
            bias_ref[t, r] = jnp.where(mine == q_doc, 0.0, NEG_BIG)
            return 0

        lax.fori_loop(0, 2 * PART, one_bias, 0)

    def bulk(pair, r, count):
        for n, (buf, dst) in enumerate(((att_o, att_hbm), (dq_o, dq_hbm))):
            for k in (1, 3, 2, 0):
                for u in pair:
                    t = u % 2
                    there = dst.at[0, pl.ds(first_round(u) + r, count), :, lanes_of(me_a(t), GROUP * DIM)]
                    b, dev = a_peer(t, k)
                    here = buf.at[u, b, pl.ds(r, count)]
                    if k:
                        remote(here, there, out_send.at[n], out_recv.at[n], dev)
                    else:
                        local(here, there, out_recv.at[n])

    def compute(pair):
        for u in pair:
            slots = key_rounds(u)[1]
            for n, buf in enumerate((qin, gin)):
                drain(buf.at[u], q_recv.at[u, n])
            for n, (buf, rest) in enumerate(((kin, (2, 3)), (vin, (1, 2)))):
                for k in rest:
                    drain(buf.at[u % 2, 0, :, slots], kvg_recv.at[u, n, k - 1])

        def one_round(u, r):
            t = u % 2
            h = me_a(t)
            here = PART * (u // 2) + r + t
            before = here - ((r + PART - 1) // PART if u == 0 else 1)

            def gain_row(g):
                return gains[pl.ds(h * GROUP + g, 1), :]

            def keys(buf, s):
                return buf[t, :, :, s].astype(F32).reshape(TOK, DIM)

            k_win = jnp.concatenate([keys(kin, here), keys(kin, before)], axis=0).astype(BF16)
            v_win = jnp.concatenate([keys(vin, here), keys(vin, before)], axis=0).astype(BF16)
            q_rows = jnp.concatenate(
                [qin[u, :, r, :, g * DIM : (g + 1) * DIM].astype(F32).reshape(SIDE * WIDE, DIM) for g in range(GROUP)],
                axis=0,
            ).astype(BF16)
            hg = jnp.concatenate(
                [
                    gin[u, :, r, :, g * DIM : (g + 1) * DIM].astype(F32).reshape(SIDE * WIDE, DIM)
                    * gain_row(g)
                    for g in range(GROUP)
                ],
                axis=0,
            ).astype(BF16)
            le = le_ref[t] > 0.5
            s_all = dot_t(k_win, q_rows)
            s = jnp.where(le, s_all[:TOK], s_all[TOK:]) * (scale * math.log2(math.e)) + bias_ref[t, PART * (u // 2) + r]
            e = jnp.exp2(s - jnp.max(s, axis=0, keepdims=True))
            p = e * (1.0 / jnp.sum(e, axis=0, keepdims=True))
            d_all = dot_t(v_win, hg)
            d = jnp.where(le, d_all[:TOK], d_all[TOK:])
            ds = p * (d - jnp.sum(p * d, axis=0, keepdims=True))
            p2 = jnp.concatenate([jnp.where(le, p, 0.0), jnp.where(le, 0.0, p)], axis=0).astype(BF16)
            ds2 = jnp.concatenate([jnp.where(le, ds, 0.0), jnp.where(le, 0.0, ds)], axis=0).astype(BF16)
            attn = dot_tn(p2, v_win).astype(BF16).astype(F32)
            dq = dot_tn(ds2, k_win) * scale
            dv = dot_n(p2, hg)
            dk = dot_n(ds2, q_rows) * scale
            for g in range(GROUP):
                rows = slice(g * SIDE * WIDE, (g + 1) * SIDE * WIDE)
                cols = slice(g * DIM, (g + 1) * DIM)
                a_g = attn[rows].reshape(SIDE, WIDE, DIM)
                gacc[t, g] += jnp.sum(a_g * gin[u, :, r, :, cols].astype(F32), axis=0)
                att_o[u, :, r, :, cols] = (a_g * gain_row(g)).astype(BF16)
                dq_o[u, :, r, :, cols] = dq[rows].reshape(SIDE, WIDE, DIM).astype(BF16)
            kp[t, :, :, before] = (kacc[t] + dk[TOK:]).reshape(SIDE, SIDE, WIDE, DIM).astype(BF16)
            vp[t, :, :, before] = (vacc[t] + dv[TOK:]).reshape(SIDE, SIDE, WIDE, DIM).astype(BF16)
            kacc[t] = dk[:TOK]
            vacc[t] = dv[:TOK]

        def both(r, _):
            for u in pair:
                one_round(u, r)
            return 0

        lax.fori_loop(0, PART, both, 0)

    def end_of_rounds():
        for t in range(2):
            last = 2 * PART - 1 + t
            kp[t, :, :, last] = kacc[t].reshape(SIDE, SIDE, WIDE, DIM).astype(BF16)
            vp[t, :, :, last] = vacc[t].reshape(SIDE, SIDE, WIDE, DIM).astype(BF16)
            for g in range(GROUP):
                gpart[t, g // 2, g % 2 : g % 2 + 1, :] = jnp.sum(gacc[t, g], axis=0, keepdims=True)

    def grad_slots(u):
        return pl.ds(*OUT_SLOTS[u])

    def sums_near(pair):
        for n, (part, got, k) in enumerate(((kp, kr, 3), (vp, vr, 1))):
            for u in pair:
                t, slots = u % 2, grad_slots(u)
                remote(
                    part.at[t, (me_g(t) + 2) % SIDE, :, slots], got.at[t, 1, :, slots],
                    rs_send.at[u, n], rs_recv.at[u, n, 1], g_peer(t, SIDE - k)[1],
                )
        for n, (part, got, k) in enumerate(((kp, kr, 3), (vp, vr, 1))):
            for u in pair:
                t, slots = u % 2, grad_slots(u)
                g, dev = g_peer(t, k)
                remote(
                    part.at[t, g, :, slots], got.at[t, 0, :, slots], rs_send.at[u, n], rs_recv.at[u, n, 0], dev
                )

    def sums_far(pair):
        for n, (part, got, k) in enumerate(((kp, kr, 1), (vp, vr, 3))):
            for u in pair:
                t, slots = u % 2, grad_slots(u)
                g, dev = g_peer(t, k)
                drain(got.at[t, 1, :, slots], rs_recv.at[u, n, 1])
                got[t, 1, :, slots] = (
                    got[t, 1, :, slots].astype(F32) + part[t, g, :, slots].astype(F32)
                ).astype(BF16)
                remote(
                    got.at[t, 1, :, slots], got.at[t, 2, :, slots], rs_send.at[u, n], rs_recv.at[u, n, 2], dev
                )

    def sums_back(pair):
        for n, (part, got, total, back) in enumerate(((kp, kr, ks, ka), (vp, vr, vs, va))):
            for u in pair:
                t, slots = u % 2, grad_slots(u)
                drain(got.at[t, 0, :, slots], rs_recv.at[u, n, 0])
                drain(got.at[t, 2, :, slots], rs_recv.at[u, n, 2])
                total[t, :, slots] = (
                    part[t, me_g(t), :, slots].astype(F32)
                    + got[t, 0, :, slots].astype(F32)
                    + got[t, 2, :, slots].astype(F32)
                ).astype(BF16)
            for k in (1, 3, 2):
                for u in pair:
                    t, slots = u % 2, grad_slots(u)
                    b, dev = a_peer(t, k)
                    remote(
                        total.at[t, b, slots], back.at[t, me_a(t), slots], aa_send.at[u, n], aa_recv.at[u, n], dev
                    )
            for u in pair:
                t, slots = u % 2, grad_slots(u)
                local(total.at[t, me_a(t), slots], back.at[t, me_a(t), slots], aa_recv.at[u, n])

    def gain_rows(go):
        @pl.when(z != x)
        def _():
            copy = pltpu.make_async_remote_copy(
                src_ref=gpart.at[0], dst_ref=ghalf.at[(z - x + 3) % SIDE], send_sem=gr_send.at[0],
                recv_sem=gr_recv.at[0], device_id=at_ctx(x * SIDE + x), device_id_type=MESH,
            )
            copy.start() if go else copy.wait_send()

        if go:
            for k in (1, 3, 2):
                i, dev = g_peer(1, k)
                remote(gpart.at[1, i], gside.at[k - 1], gr_send.at[1], gr_recv.at[1], dev)
        else:
            drain(gpart.at[1, pl.ds(0, SIDE - 1)], gr_send.at[1])

    def gain_cols(go):
        @pl.when(z == x)
        def _():
            if go:
                drain(ghalf, gr_recv.at[0])
                gsum[...] = gpart[0] + ghalf[0] + ghalf[1] + ghalf[2]
                for k in (1, 3, 2):
                    i, dev = g_peer(1, k)
                    remote(gsum.at[i], gdiag, ga_send, ga_recv, dev)
                gdiag[...] = gsum[x]
            else:
                drain(gsum.at[pl.ds(0, SIDE - 1)], ga_send)

    def gain_over_dp():
        drain(gside, gr_recv.at[1])

        @pl.when(z != x)
        def _():
            drain(gdiag, ga_recv)

        gfin[...] = gdiag[...] + gpart[1, x] + gside[0] + gside[1] + gside[2]
        for i in range(1, 8):
            remote(gfin, gdp.at[i - 1], d_send, d_recv, ((dp + i) % 8, ctx))

    def finish(pair):
        for n, (back, out) in enumerate(((ka, dk_ref), (va, dv_ref))):
            for u in pair:
                t = u % 2
                drain(back.at[t, :, grad_slots(u)], aa_recv.at[u, n])
            for u in pair:
                t = u % 2
                start, count = OUT_SLOTS[u]
                for slot in range(start, start + count):
                    rho = slot + (2 * PART - 1) * t
                    if t == 1 and slot == 0:
                        continue
                    for h in range(HEADS):
                        val = back[t, h, slot]
                        if t == 0 and slot == 2 * PART - 1:
                            val = (val.astype(F32) + back[1, h, 0].astype(F32)).astype(BF16)
                        out[0, rho, :, h * DIM : (h + 1) * DIM] = val

    kacc[...] = jnp.zeros_like(kacc)
    vacc[...] = jnp.zeros_like(vacc)
    gacc[...] = jnp.zeros_like(gacc)
    compute(first)
    sums_near(first)
    bulk(first, 0, PART)
    compute(second)
    end_of_rounds()
    sums_near(second)
    gain_rows(True)
    sums_far(first)
    bulk(second, 0, 1)
    sums_far(second)
    gain_cols(True)
    sums_back(first)
    bulk(second, 1, 1)

    @pl.when(dp < 7)
    def _():
        pl.semaphore_wait(hello, 7 - dp)

    gain_over_dp()
    sums_back(second)
    bulk(second, 2, 2)
    finish(first)
    finish(second)
    drain(gdp, d_recv)
    total = gfin[...]
    for i in range(7):
        total += gdp[i]
    for i in range(2):
        gg_ref[pl.ds(i * DIM, DIM)] = total[i] * (1.0 / 128.0)
    for u in range(4):
        t, slots, grads = u % 2, key_rounds(u)[1], grad_slots(u)
        for n, buf in enumerate((kin, vin)):
            drain(buf.at[t, 0, pl.ds(0, SIDE - 1), slots], kv_send.at[u, n])
            drain(buf.at[t, pl.ds(0, SIDE - 1), :, slots], kvg_send.at[u, n])
        for n, (got, back) in enumerate(((kr, ka), (vr, va))):
            drain(got.at[t, :, :, grads], rs_send.at[u, n])
            drain(back.at[t, pl.ds(0, SIDE - 1), grads], aa_send.at[u, n])
    for n, buf in enumerate((qin, gin)):
        drain(buf.at[:, pl.ds(0, SIDE - 1)], q_send.at[n])
    for n, (buf, dst) in enumerate(((att_o, att_hbm), (dq_o, dq_hbm))):
        drain(buf.at[:, pl.ds(0, SIDE - 1)], out_send.at[n])
        drain(dst, out_recv.at[n])
    gain_rows(False)
    gain_cols(False)
    drain(gdp, d_send)


def write_out(att, dq, dk, dv, gg, att_out, dq_out, dk_out, dv_out, gg_out, big, small):
    copies = []
    for n, (src, dst) in enumerate(((att, att_out), (dq, dq_out))):
        for i in range(4):
            part = pl.ds(i * 4, 4)
            copies.append(pltpu.make_async_copy(src.at[:, part], dst.at[:, part], big.at[n, i]))
    for n, (src, dst) in enumerate(((dk, dk_out), (dv, dv_out), (gg, gg_out))):
        copies.append(pltpu.make_async_copy(src, dst, small.at[n]))
    for copy in copies:
        copy.start()
    for copy in copies:
        copy.wait()


def body(queries, key_rows, values, out_grad, out_gain, documents):
    queries, key_rows, values, out_grad, out_gain, documents = (
        pltpu.with_memory_space_constraint(a, pltpu.HBM)
        for a in (queries, key_rows, values, out_grad, out_gain, documents)
    )
    any_spec = pl.BlockSpec(memory_space=pl.ANY)
    vmem = pl.BlockSpec(memory_space=pltpu.VMEM)
    wide = pltpu.VMEM((4, SIDE, PART, WIDE, GROUP * DIM), BF16)
    narrow = pltpu.VMEM((2, SIDE, SIDE, SLOTS, WIDE, DIM), BF16)
    narrow3 = pltpu.VMEM((2, SIDE - 1, SIDE, SLOTS, WIDE, DIM), BF16)
    flat = pltpu.VMEM((2, SIDE, SLOTS, WIDE, DIM), BF16)
    dma = pltpu.SemaphoreType.DMA
    att, dq, dk, dv, gg = pl.pallas_call(
        kernel,
        out_shape=(
            jax.ShapeDtypeStruct(queries.shape, BF16),
            jax.ShapeDtypeStruct(queries.shape, BF16),
            jax.ShapeDtypeStruct(key_rows.shape, BF16),
            jax.ShapeDtypeStruct(key_rows.shape, BF16),
            jax.ShapeDtypeStruct((2 * DIM,), F32),
        ),
        in_specs=[any_spec] * 6,
        out_specs=(any_spec, any_spec, vmem, vmem, vmem),
        scratch_shapes=[
            wide, wide, narrow, narrow, wide, wide, narrow, narrow, narrow3, narrow3, flat, flat, flat, flat,
            pltpu.VMEM((2, 4, ROUNDS, WIDE, DIM), BF16),
            pltpu.VMEM(out_gain.shape, BF16),
            pltpu.VMEM(documents.shape, jnp.int32),
            pltpu.VMEM((2, TOK, ROWS), F32),
            pltpu.VMEM((2, 2 * PART, TOK, ROWS), F32),
            pltpu.VMEM((2, TOK, DIM), F32),
            pltpu.VMEM((2, TOK, DIM), F32),
            pltpu.VMEM((2, GROUP, WIDE, DIM), F32),
            pltpu.VMEM((HEADS * GROUP, DIM), F32),
            pltpu.VMEM((2, SIDE, 2, DIM), F32),
            pltpu.VMEM((SIDE - 1, SIDE, 2, DIM), F32),
            pltpu.VMEM((SIDE, 2, DIM), F32),
            pltpu.VMEM((SIDE - 1, 2, DIM), F32),
            pltpu.VMEM((2, DIM), F32),
            pltpu.VMEM((2, DIM), F32),
            pltpu.VMEM((7, 2, DIM), F32),
            dma((4, 2)), dma((4, 2)), dma((4, 2)), dma((4, 2, 3)), dma((2,)), dma((4, 2)), dma((2,)), dma((2,)),
            dma((4, 2)), dma((4, 2, 3)), dma((4, 2)), dma((4, 2)), dma((2,)), dma((2,)), dma, dma, dma, dma,
            dma((2,)), pltpu.SemaphoreType.REGULAR, dma,
        ],
        compiler_params=pltpu.CompilerParams(
            collective_id=0, has_side_effects=True, vmem_limit_bytes=48 * 1024 * 1024
        ),
        name="packed_attention",
    )(queries, key_rows, values, out_grad, out_gain, documents)
    return pl.pallas_call(
        write_out,
        out_shape=(
            jax.ShapeDtypeStruct(queries.shape, BF16),
            jax.ShapeDtypeStruct(queries.shape, BF16),
            jax.ShapeDtypeStruct(key_rows.shape, BF16),
            jax.ShapeDtypeStruct(key_rows.shape, BF16),
            jax.ShapeDtypeStruct((2 * DIM,), F32),
        ),
        in_specs=[any_spec] * 5,
        out_specs=(any_spec,) * 5,
        scratch_shapes=[dma((2, 4)), dma((3,))],
        compiler_params=pltpu.CompilerParams(vmem_limit_bytes=1024 * 1024),
        name="write_out",
    )(att, dq, dk, dv, gg)


def solution(mesh):
    tokens = P("dp", None, "ctx", None)
    return jax.shard_map(
        body,
        mesh=mesh,
        in_specs=(tokens, tokens, tokens, tokens, P(), P("dp", None)),
        out_specs=(tokens, tokens, tokens, tokens, P("ctx")),
        check_vma=False,
    )
```

time: 49.4 us -> 47.1 us (0.953)
  Pallas kernels: 48.6 us -> 46.3 us
    pallas_call x1, Pallas kernels: 46.6 us -> 44.8 us  [body(): pl.pallas_call(kernel, out_shape=(jax.ShapeDtypeStruct(queries.shape, BF1...]
    pallas_call x1, Pallas kernels: 2.04 us -> 1.5 us  [body(): pl.pallas_call(write_out, out_shape=(jax.ShapeDtypeStruct(queries.shape,...]
where the time goes in v4:
time: 47.1 us; the launch traced here: 47 us
  Pallas kernels  46.3 us (98%)
  between operations  0.64 us (1%)
    pallas_call x1, Pallas kernels, body(): pl.pallas_call(kernel, out_shape=(jax.ShapeDtypeStruct(queries.shape, BF1...  44.8 us
    pallas_call x1, Pallas kernels, body(): pl.pallas_call(write_out, out_shape=(jax.ShapeDtypeStruct(queries.shape,...  1.5 us

profile of v4, /device:TPU:0, one launch (start us, length us, event | category | flops | bytes accessed | tf_op | source)
XLA Modules:
  0.0 47.0 jit_solution(12083070688426680526)
XLA Ops:
  0.6 44.8 %packed_attention.1 = (bf16[1,16,8,4096]{3,2,1,0:T(8,128)(2,1)S(1)}, bf16[1,16,8,4096]{3,2,1,0:T(8,128)(2,1)S(1)}, bf16[1,16,8,512]{3,2,1,0:T(8,128)(2,1)S(1)}, ...) custom-call(bf16[1,16,8,4096]{3,2,1,0:T(8,128)(2,1)} %q_hbm.1, bf16[1,16,8,512]{3,2,1,0:T(8,128)(2,1)} %k_hbm.1, ...), custom_call_target="tpu_custom_call" | custom-call | tf_op jit(solution)/shard_map/packed_attention/pallas_call | solution.py:509
  45.5 1.5 %write_out.1 = (bf16[1,16,8,4096]{3,2,1,0:T(8,128)(2,1)}, bf16[1,16,8,4096]{3,2,1,0:T(8,128)(2,1)}, bf16[1,16,8,512]{3,2,1,0:T(8,128)(2,1)}, bf16[1,16,8,512]{3,2,1,0:T(8,128)(2,1)}, f32[256]{0:T(256)}) custom-call(bf16[1,16,8,4096]{3,2,1,0:T(8,128)(2,1)S(1)} %get-tuple-element.10.att, bf16[1,16,8,4096]{3,2,1,0:T(8,128)(2,1)S(1)} %get-tuple-element.11.dq, ...), custom_call_target="tpu_custom_call" | custom-call | tf_op jit(solution)/shard_map/write_out/pallas_call | solution.py:547

commit v5 on v4

--- a/solution.py
+++ b/solution.py
@@ -55,19 +55,31 @@
     def at_ctx(c):
         return (dp, c)
 
+    core = dp % 2
+
+    def over_x(t):
+        return 1 - core if t == 0 else core
+
+    def me_a(t):
+        return over_x(t) * x + (1 - over_x(t)) * z
+
+    def me_g(t):
+        return over_x(t) * z + (1 - over_x(t)) * x
+
+    def device(t, a, g):
+        return at_ctx(over_x(t) * (g * SIDE + a) + (1 - over_x(t)) * (a * SIDE + g))
+
     def a_peer(t, k):
-        a = ((x if t == 0 else z) + k) % SIDE
-        return a, at_ctx(z * SIDE + a if t == 0 else a * SIDE + x)
+        a = (me_a(t) + k) % SIDE
+        return a, device(t, a, me_g(t))
 
     def g_peer(t, k):
-        g = ((z if t == 0 else x) + k) % SIDE
-        return g, at_ctx(g * SIDE + x if t == 0 else z * SIDE + g)
-
-    def me_a(t):
-        return x if t == 0 else z
-
-    def me_g(t):
-        return z if t == 0 else x
+        g = (me_g(t) + k) % SIDE
+        return g, device(t, me_a(t), g)
+
+    def x_peer(k):
+        i = (x + k) % SIDE
+        return i, at_ctx(z * SIDE + i)
 
     def first_round(u):
         return 2 * PART * (u % 2) + PART * (u // 2)
@@ -194,12 +206,14 @@
     key_i = lax.broadcasted_iota(jnp.int32, (TOK, ROWS), 0)
     row_i = lax.broadcasted_iota(jnp.int32, (TOK, ROWS), 1) & (SIDE * WIDE - 1)
     for t in range(2):
+        a_step = WIDE * over_x(t) + WIDE * SIDE * (1 - over_x(t))
+        g_step = WIDE * (1 + SIDE) - a_step
+
         def key_col(i):
-            return i if t == 0 else ((i >> 3) & 3) * 32 + (i >> 5) * 8 + (i & 7)
+            return ((i >> 3) & 3) * a_step + (i >> 5) * g_step + (i & 7)
 
         def row_col(i):
-            i = i & (SIDE * WIDE - 1)
-            return z * 32 + i if t == 0 else (i >> 3) * 32 + x * 8 + (i & 7)
+            return ((i >> 3) & 3) * a_step + me_g(t) * g_step + (i & 7)
 
         le = key_col(key_i) <= row_col(row_i)
         le_ref[t] = jnp.where(le, 1.0, 0.0)
@@ -376,15 +390,15 @@
         @pl.when(z != x)
         def _():
             copy = pltpu.make_async_remote_copy(
-                src_ref=gpart.at[0], dst_ref=ghalf.at[(z - x + 3) % SIDE], send_sem=gr_send.at[0],
+                src_ref=gpart.at[core], dst_ref=ghalf.at[(z - x + 3) % SIDE], send_sem=gr_send.at[0],
                 recv_sem=gr_recv.at[0], device_id=at_ctx(x * SIDE + x), device_id_type=MESH,
             )
             copy.start() if go else copy.wait_send()
 
         if go:
             for k in (1, 3, 2):
-                i, dev = g_peer(1, k)
-                remote(gpart.at[1, i], gside.at[k - 1], gr_send.at[1], gr_recv.at[1], dev)
+                i, dev = x_peer(k)
+                remote(gpart.at[1 - core, i], gside.at[k - 1], gr_send.at[1], gr_recv.at[1], dev)
         else:
             drain(gpart.at[1, pl.ds(0, SIDE - 1)], gr_send.at[1])
 
@@ -393,9 +407,9 @@
         def _():
             if go:
                 drain(ghalf, gr_recv.at[0])
-                gsum[...] = gpart[0] + ghalf[0] + ghalf[1] + ghalf[2]
+                gsum[...] = gpart[core] + ghalf[0] + ghalf[1] + ghalf[2]
                 for k in (1, 3, 2):
-                    i, dev = g_peer(1, k)
+                    i, dev = x_peer(k)
                     remote(gsum.at[i], gdiag, ga_send, ga_recv, dev)
                 gdiag[...] = gsum[x]
             else:
@@ -408,7 +422,7 @@
         def _():
             drain(gdiag, ga_recv)
 
-        gfin[...] = gdiag[...] + gpart[1, x] + gside[0] + gside[1] + gside[2]
+        gfin[...] = gdiag[...] + gpart[1 - core, x] + gside[0] + gside[1] + gside[2]
         for i in range(1, 8):
             remote(gfin, gdp.at[i - 1], d_send, d_recv, ((dp + i) % 8, ctx))
 
@@ -438,20 +452,20 @@
     bulk(first, 0, PART)
     compute(second)
     end_of_rounds()
+    gain_rows(True)
     sums_near(second)
-    gain_rows(True)
     sums_far(first)
+    gain_cols(True)
     bulk(second, 0, 1)
     sums_far(second)
-    gain_cols(True)
     sums_back(first)
-    bulk(second, 1, 1)
 
     @pl.when(dp < 7)
     def _():
         pl.semaphore_wait(hello, 7 - dp)
 
     gain_over_dp()
+    bulk(second, 1, 1)
     sums_back(second)
     bulk(second, 2, 2)
     finish(first)

time: 47.1 us -> 46.9 us (level)
  no operation moved by 1% of the time
where the time goes in v5:
time: 46.9 us; the launch traced here: 46.7 us
  Pallas kernels  46.1 us (98%)
  between operations  0.64 us (1%)
    pallas_call x1, Pallas kernels, body(): pl.pallas_call(kernel, out_shape=(jax.ShapeDtypeStruct(queries.shape, BF1...  44.6 us
    pallas_call x1, Pallas kernels, body(): pl.pallas_call(write_out, out_shape=(jax.ShapeDtypeStruct(queries.shape,...  1.5 us

profile of v5, /device:TPU:0, one launch (start us, length us, event | category | flops | bytes accessed | tf_op | source)
XLA Modules:
  0.0 46.7 jit_solution(6836130146144237538)
XLA Ops:
  0.6 44.6 %packed_attention.1 = (bf16[1,16,8,4096]{3,2,1,0:T(8,128)(2,1)S(1)}, bf16[1,16,8,4096]{3,2,1,0:T(8,128)(2,1)S(1)}, bf16[1,16,8,512]{3,2,1,0:T(8,128)(2,1)S(1)}, ...) custom-call(bf16[1,16,8,4096]{3,2,1,0:T(8,128)(2,1)} %q_hbm.1, bf16[1,16,8,512]{3,2,1,0:T(8,128)(2,1)} %k_hbm.1, ...), custom_call_target="tpu_custom_call" | custom-call | tf_op jit(solution)/shard_map/packed_attention/pallas_call | solution.py:523
  45.2 1.5 %write_out.1 = (bf16[1,16,8,4096]{3,2,1,0:T(8,128)(2,1)}, bf16[1,16,8,4096]{3,2,1,0:T(8,128)(2,1)}, bf16[1,16,8,512]{3,2,1,0:T(8,128)(2,1)}, bf16[1,16,8,512]{3,2,1,0:T(8,128)(2,1)}, f32[256]{0:T(256)}) custom-call(bf16[1,16,8,4096]{3,2,1,0:T(8,128)(2,1)S(1)} %get-tuple-element.10.att, bf16[1,16,8,4096]{3,2,1,0:T(8,128)(2,1)S(1)} %get-tuple-element.11.dq, ...), custom_call_target="tpu_custom_call" | custom-call | tf_op jit(solution)/shard_map/write_out/pallas_call | solution.py:561
